TPU v7x, 512 devices: a whole 4x4x16 slice. The times are simulated.
512 devices in a mesh: rep: 4 (over y), dev: 128 (over z, x, core).
Axes of the slice: x: 4, y: 4, z: 16, core: 2. Of those that a mesh axis runs over, the one named last changes fastest.
Arguments:
- params: float32 [59, 65536], P(None, 'dev'), may hold values from -12 to 24, as said below
- adam_m: float32 [59, 65536], P(None, 'dev'), may hold values from -0.6 to 0.6
- adam_v: float32 [59, 65536], P(None, 'dev'), may hold values from 0.001 to 0.1
- target: float32 [4, 128, 2, 3, 256], P('rep', 'dev'), may hold values from 0 to 1
- tile_ids: int32 [4, 128, 2], P('rep', 'dev'), may hold values from 0 to 1023, as said below
- send_blocks: int32 [4, 128, 128, 1], P('rep', 'dev'), may hold values from -1 to 7, as said below
- tile_lists: int32 [4, 128, 2, 8], P('rep', 'dev'), may hold values from -1 to 127, as said below
Outputs:
- new_params: float32 [59, 65536], P(None, 'dev')
- new_m: float32 [59, 65536], P(None, 'dev')
- new_v: float32 [59, 65536], P(None, 'dev')
- grad: float32 [59, 65536], P(None, 'dev')
Inputs may be any that keep to these rules, and one draw needn't show every extreme that they name: `tile_ids`: every tile of the 64 x 8 region of each view is assigned to exactly one device. `send_blocks`: A value is view * 4 + block of the owner, or -1 where the owner provides nothing in that slot; the view of every live value equals the view of that renderer's tiles; the live values of one owner for one renderer are distinct blocks. `tile_lists`: A list is either all -1 or holds 8 live entries, front to back; every live entry names a slot whose send_blocks entry for this renderer is live, and the live entries of one renderer are distinct. `params`: row 2 lies in [18, 22], row 10 is at most 1, the quaternion rows have norm at least 0.5.
All inputs are finite; a program needn't handle non-finite values.
Results may differ from a plain program's by a relative error of at most 0.0003.
Values sent between devices are 32-bit elements; how exact they have to be, the bound alone decides.
No kernel may reach another device: no remote copies, remote signals or barrier semaphores. Data moves between devices by JAX's collectives and lax.ppermute only.
A program may use at most 64 MiB of HBM per device.

v0:
```python
import jax
import jax.numpy as jnp
from jax import lax
from jax.sharding import PartitionSpec as P

BLOCK = 128
PARAMS = 59
TILES_X = 64
ADAM_STEP = 1000


FOCAL = 1100.0
DEPTH_ZERO = 20.0
BASELINE = 16.0 * DEPTH_ZERO / FOCAL
BLUR = 0.3
SMOOTHING = 0.0001
BETA_ONE = 0.9
BETA_TWO = 0.999
ADAM_EPS = 1e-15
SH_ZERO = 0.28209479177387814
SH_ONE = 0.4886025119029199
SH_TWO = [
    1.0925484305920792,
    -1.0925484305920792,
    0.31539156525252005,
    -1.0925484305920792,
    0.5462742152960396,
]
SH_THREE = [
    -0.5900435899266435,
    2.890611442640554,
    -0.4570457994644658,
    0.3731763325901154,
    -0.4570457994644658,
    1.445305721320277,
    -0.5900435899266435,
]
RATE_LIST = [0.00016] * 3 + [0.005] * 3 + [0.001] * 4 + [0.05] + [0.0025] * 3 + [0.000125] * 45


def sh_basis(unit_x, unit_y, unit_z):
    square_x = unit_x * unit_x
    square_y = unit_y * unit_y
    square_z = unit_z * unit_z
    return [
        SH_ZERO + 0.0 * unit_x,
        -SH_ONE * unit_y,
        SH_ONE * unit_z,
        -SH_ONE * unit_x,
        SH_TWO[0] * unit_x * unit_y,
        SH_TWO[1] * unit_y * unit_z,
        SH_TWO[2] * (2.0 * square_z - square_x - square_y),
        SH_TWO[3] * unit_x * unit_z,
        SH_TWO[4] * (square_x - square_y),
        SH_THREE[0] * unit_y * (3.0 * square_x - square_y),
        SH_THREE[1] * unit_x * unit_y * unit_z,
        SH_THREE[2] * unit_y * (4.0 * square_z - square_x - square_y),
        SH_THREE[3] * unit_z * (2.0 * square_z - 3.0 * square_x - 3.0 * square_y),
        SH_THREE[4] * unit_x * (4.0 * square_z - square_x - square_y),
        SH_THREE[5] * unit_z * (square_x - square_y),
        SH_THREE[6] * unit_x * (square_x - 3.0 * square_y),
    ]


def project(raw_rows, baseline_shift, center_x, center_y):
    offset_x = raw_rows[0] - baseline_shift
    offset_y = raw_rows[1]
    depth = raw_rows[2]
    inverse = 1.0 / depth
    focal_depth = FOCAL * inverse
    screen_x = focal_depth * offset_x + center_x
    screen_y = focal_depth * offset_y + center_y
    scales = jnp.exp(raw_rows[3:6])
    quaternion = raw_rows[6:10]
    quaternion = quaternion / jnp.sqrt(jnp.sum(quaternion * quaternion, axis=0))
    quat_w, quat_x, quat_y, quat_z = (quaternion[0], quaternion[1], quaternion[2], quaternion[3])
    rotation = [
        [
            1.0 - 2.0 * (quat_y * quat_y + quat_z * quat_z),
            2.0 * (quat_x * quat_y - quat_w * quat_z),
            2.0 * (quat_x * quat_z + quat_w * quat_y),
        ],
        [
            2.0 * (quat_x * quat_y + quat_w * quat_z),
            1.0 - 2.0 * (quat_x * quat_x + quat_z * quat_z),
            2.0 * (quat_y * quat_z - quat_w * quat_x),
        ],
        [
            2.0 * (quat_x * quat_z - quat_w * quat_y),
            2.0 * (quat_y * quat_z + quat_w * quat_x),
            1.0 - 2.0 * (quat_x * quat_x + quat_y * quat_y),
        ],
    ]
    slope_x = focal_depth * offset_x * inverse
    slope_y = focal_depth * offset_y * inverse
    first_row = [
        (focal_depth * rotation[0][index] - slope_x * rotation[2][index]) * scales[index]
        for index in range(3)
    ]
    second_row = [
        (focal_depth * rotation[1][index] - slope_y * rotation[2][index]) * scales[index]
        for index in range(3)
    ]
    sigma_xx = (
        first_row[0] * first_row[0]
        + first_row[1] * first_row[1]
        + first_row[2] * first_row[2]
        + BLUR
    )
    sigma_xy = (
        first_row[0] * second_row[0] + first_row[1] * second_row[1] + first_row[2] * second_row[2]
    )
    sigma_yy = (
        second_row[0] * second_row[0]
        + second_row[1] * second_row[1]
        + second_row[2] * second_row[2]
        + BLUR
    )
    determinant = sigma_xx * sigma_yy - sigma_xy * sigma_xy
    opacity = jax.nn.sigmoid(raw_rows[10])
    distance = jnp.sqrt(offset_x * offset_x + offset_y * offset_y + depth * depth)
    basis = jnp.stack(sh_basis(offset_x / distance, offset_y / distance, depth / distance))
    coeffs = raw_rows[11:].reshape(16, 3, raw_rows.shape[1])
    color = jnp.maximum(jnp.sum(basis[:, None, :] * coeffs, axis=0) + 0.5, 0.0)
    screen = jnp.stack(
        [
            screen_x,
            screen_y,
            sigma_yy / determinant,
            -sigma_xy / determinant,
            sigma_xx / determinant,
            opacity,
        ]
    )
    return jnp.concatenate([screen, color], axis=0)


def blocked_prefix(survive):
    pixels, width = survive.shape
    grouped = survive.reshape(pixels, width // BLOCK, BLOCK)
    lanes = jnp.arange(BLOCK, dtype=jnp.int32)
    upper = (lanes[:, None] < lanes[None, :]).astype(jnp.float32)
    inner = jnp.einsum("pnk,ki->pni", grouped, upper, precision=lax.Precision.HIGHEST)
    totals = jnp.sum(grouped, axis=2)
    before = jnp.cumsum(totals, axis=1) - totals
    return (inner + before[:, :, None]).reshape(pixels, width)


def render_loss(features, gaussian_mask, anchor_x, anchor_y, goal_tile, prefix_fn):
    pixels = jnp.arange(goal_tile.shape[1], dtype=jnp.int32)
    pixel_x = anchor_x + (pixels % 16).astype(jnp.float32) + 0.5
    pixel_y = anchor_y + (pixels // 16).astype(jnp.float32) + 0.5
    delta_x = pixel_x[:, None] - features[0][None, :]
    delta_y = pixel_y[:, None] - features[1][None, :]
    power = (
        -0.5 * (features[2] * delta_x * delta_x + features[4] * delta_y * delta_y)
        - features[3] * delta_x * delta_y
    )
    alpha = features[5] * jnp.exp(power) * gaussian_mask
    survive = jnp.log(1.0 - alpha)
    weight = alpha * jnp.exp(prefix_fn(survive))
    color = jnp.einsum("ck,pk->cp", features[6:9], weight, precision=lax.Precision.HIGHEST)
    error = color - goal_tile
    return jnp.sum(jnp.sqrt(error * error + SMOOTHING)) / 3.0


def accumulate(incoming, items, center_x, center_y):

    def tile_grad(total, item):
        slot_ids, block_mask, baseline_shift, corner_x, corner_y, goal_tile = item
        chosen = incoming[slot_ids]

        def loss_of(blocks):
            flat = blocks.transpose(1, 0, 2).reshape(blocks.shape[1], blocks.shape[0] * BLOCK)
            flat = project(flat, baseline_shift, center_x, center_y)
            return render_loss(
                flat, jnp.repeat(block_mask, BLOCK), corner_x, corner_y, goal_tile, blocked_prefix
            )

        _, back = jax.vjp(loss_of, chosen)
        grads = back(jnp.ones((), jnp.float32))[0]
        return (total.at[slot_ids].add(grads), None)

    total, _ = lax.scan(tile_grad, jnp.zeros_like(incoming), items)
    return total


def collect(returned, row_index, live_rows, row_count):
    rows_all = jnp.arange(row_count, dtype=jnp.int32)
    picker = ((row_index[None, :] == rows_all[:, None]) & live_rows[None, :]).astype(jnp.float32)
    return jnp.einsum("bn,nfk->bfk", picker, returned, precision=lax.Precision.HIGHEST)


def adam_update(params, adam_m, adam_v, grad):
    new_m = BETA_ONE * adam_m + (1.0 - BETA_ONE) * grad
    new_v = BETA_TWO * adam_v + (1.0 - BETA_TWO) * grad * grad
    m_hat = new_m / (1.0 - BETA_ONE**ADAM_STEP)
    v_hat = new_v / (1.0 - BETA_TWO**ADAM_STEP)
    rates = jnp.array(RATE_LIST, jnp.float32)[:, None]
    return (params - rates * m_hat / (jnp.sqrt(v_hat) + ADAM_EPS), new_m, new_v)


def on_device(params, adam_m, adam_v, target, tile_ids, send_blocks, tile_lists):
    dev_count = lax.axis_size("dev")
    g_local = params.shape[1]
    blocks_here = g_local // BLOCK
    tiles_y = dev_count * blocks_here // TILES_X
    center_x = 8.0 * TILES_X
    center_y = 8.0 * tiles_y
    per_view = TILES_X * tiles_y
    tile_nums = tile_ids[0, 0]
    lists = tile_lists[0, 0]
    goals = target[0, 0]
    views = tile_nums // per_view
    within = tile_nums % per_view
    shifts = views.astype(jnp.float32) * BASELINE
    anchor_x = (within % TILES_X * 16).astype(jnp.float32)
    anchor_y = (within // TILES_X * 16).astype(jnp.float32)
    masks = (lists >= 0).astype(jnp.float32)
    slots = jnp.maximum(lists, 0)
    items = (slots, masks, shifts, anchor_x, anchor_y, goals)
    provided = send_blocks[0, 0].reshape(-1)
    live_rows = provided >= 0
    local_block = jnp.where(live_rows, provided % blocks_here, 0)
    raw_blocks = params.reshape(PARAMS, blocks_here, BLOCK).transpose(1, 0, 2)
    outgoing = raw_blocks[local_block]
    incoming = lax.all_to_all(outgoing, "dev", split_axis=0, concat_axis=0, tiled=True)
    cotangent = accumulate(incoming, items, center_x, center_y)
    returned = lax.all_to_all(cotangent, "dev", split_axis=0, concat_axis=0, tiled=True)
    per_block = collect(returned, local_block, live_rows, blocks_here)
    grad = per_block.transpose(1, 0, 2).reshape(PARAMS, g_local)
    grad = lax.psum(grad, "rep")
    new_params, new_m, new_v = adam_update(params, adam_m, adam_v, grad)
    return (new_params, new_m, new_v, grad)


def solution(mesh):
    placed = (
        P(None, "dev"),
        P(None, "dev"),
        P(None, "dev"),
        P("rep", "dev", None, None, None),
        P("rep", "dev", None),
        P("rep", "dev", None, None),
        P("rep", "dev", None, None),
    )
    return jax.shard_map(
        on_device,
        mesh=mesh,
        in_specs=placed,
        out_specs=(P(None, "dev"), P(None, "dev"), P(None, "dev"), P(None, "dev")),
        check_vma=False,
    )
```

profile of v0, /device:TPU:6, one launch (start us, length us, event | category | flops | bytes accessed | tf_op | source)
XLA Modules:
  0.0 579.4 jit_solution(773480621831141070)
XLA Ops:
  8.8 2.8 gather_fusion.1
  11.6 20.0 %all-to-all-start = ((f32[128,59,128]{2,1,0:T(8,128)}), f32[128,59,128]{2,1,0:T(8,128)}, u32[]{:S(2)}, u32[]{:S(2)}) async-start(f32[128,59,128]{2,1,0:T(8,128)} %gather_fusion.1), calls=%async_computation | async-start | bytes 8388608 | tf_op jit(solution)/shard_map/all_to_all | solution.py:227
  32.3 185.2 %all-to-all-done = f32[128,59,128]{2,1,0:T(8,128)} async-done(((f32[128,59,128]{2,1,0:T(8,128)}), f32[128,59,128]{2,1,0:T(8,128)}, u32[]{:S(2)}, u32[]{:S(2)}) %all-to-all-start) | async-done | bytes 3866656 | tf_op jit(solution)/shard_map/all_to_all | solution.py:227
  217.5 2.5 broadcast_in_dim.73
  220.0 93.3 %while.12 = (s32[]{:T(128)}, f32[128,59,128]{2,1,0:T(8,128)}, s32[2,8]{1,0:T(2,128)}, f32[128,59,128]{2,1,0:T(8,128)}, f32[2]{0:T(128)S(1)}, /*index=5*/f32[2]{0...) while((s32[]{:T(128)}, f32[128,59,128]{2,1,0:T(8,128)}, ...), condition=%wide.region_16.17_spmd, body=%wide.region_0.16_spmd.sunk | while | flops 866936576 | bytes 31245920 | solution.py:184
  220.7 2.8 gather_fusion
  242.0 1.6 negate_add_fusion.4
  244.6 1.7 convolution_add_fusion.3
  248.2 1.8 fusion.200
  250.1 1.9 fusion.201
  254.3 1.8 fusion.203
  264.3 2.3 scatter_fusion
  267.3 2.8 gather_fusion
  288.6 1.6 negate_add_fusion.4
  291.2 1.7 convolution_add_fusion.3
  294.8 1.8 fusion.200
  296.7 1.9 fusion.201
  300.8 1.8 fusion.203
  310.8 2.3 scatter_fusion
  313.4 11.2 %all-to-all-start.1 = ((f32[128,59,128]{2,1,0:T(8,128)}), f32[128,59,128]{2,1,0:T(8,128)}, u32[]{:S(2)}, u32[]{:S(2)}) async-start(f32[128,59,128]{2,1,0:T(8,128)} %get-tuple-element.121), calls=%async_computation.1 | async-start | bytes 8388608 | tf_op jit(solution)/shard_map/all_to_all | solution.py:229
  324.8 185.7 %all-to-all-done.1 = f32[128,59,128]{2,1,0:T(8,128)} async-done(((f32[128,59,128]{2,1,0:T(8,128)}), f32[128,59,128]{2,1,0:T(8,128)}, u32[]{:S(2)}, u32[]{:S(2)}) %all-to-all-start.1) | async-done | bytes 3866656 | tf_op jit(solution)/shard_map/all_to_all | solution.py:229
  510.5 5.5 fusion.121
  516.7 52.5 %all-reduce.26.cloned.1.call-done = f32[59,512]{1,0:T(8,128)} async-done(((f32[59,512]{1,0:T(8,128)}), f32[59,512]{1,0:T(8,128)}) %all-reduce.26.cloned.1.call-update) | async-done | bytes 120848 | tf_op jit(solution)/shard_map/psum | solution.py:232
  569.3 1.7 divide_subtract_fusion
  (477 shorter events, 67.3 us)
Async XLA Ops:
  11.6 20.0 %copy-start.73 = (f32[1,1,2,3,256]{4,2,3,1,0:T(2,128)S(1)}, f32[1,1,2,3,256]{4,2,3,1,0:T(2,128)}, u32[]{:S(2)}) copy-start(f32[1,1,2,3,256]{4,2,3,1,0:T(2,128)} %param.13) | copy-start | bytes 18436
  11.6 20.0 %copy-start.78 = (s32[1,1,2]{2,1,0:T(1,128)S(1)}, s32[1,1,2]{2,1,0:T(1,128)}, u32[]{:S(2)}) copy-start(s32[1,1,2]{2,1,0:T(1,128)} %param.14) | copy-start | bytes 28
  11.6 20.1 %copy-start.74 = (s32[1,1,2,8]{3,2,1,0:T(2,128)S(1)}, s32[1,1,2,8]{3,2,1,0:T(2,128)}, u32[]{:S(2)}) copy-start(s32[1,1,2,8]{3,2,1,0:T(2,128)} %param.16) | copy-start | bytes 196
  11.6 205.8 %all-to-all-start = ((f32[128,59,128]{2,1,0:T(8,128)}), f32[128,59,128]{2,1,0:T(8,128)}, u32[]{:S(2)}, u32[]{:S(2)}) async-start(f32[128,59,128]{2,1,0:T(8,128)} %gather_fusion.1), calls=%async_computation | async-start | bytes 8388608 | tf_op jit(solution)/shard_map/all_to_all | solution.py:227
  220.0 13.9 %copy-start.71 = (f32[2,3,256]{2,1,0:T(4,128)}, f32[2,3,256]{2,1,0:T(4,128)S(1)}, u32[]{:S(2)}) copy-start(f32[2,3,256]{2,1,0:T(4,128)S(1)} %get-tuple-element.527) | copy-start | bytes 18436 | tf_op jit(solution)/shard_map/while
  250.1 14.2 %copy-start.70 = (s32[8]{0:T(128)S(1)}, s32[8]{0:T(128)}, u32[]{:S(2)}) copy-start(s32[8]{0:T(128)} %copy-done.69) | copy-start | bytes 100 | tf_op jit(solution)/shard_map/while
  250.1 16.4 %copy-start.72 = (f32[2,3,256]{2,1,0:T(4,128)S(1)}, f32[2,3,256]{2,1,0:T(4,128)}, u32[]{:S(2)}) copy-start(f32[2,3,256]{2,1,0:T(4,128)} %copy-done.71) | copy-start | bytes 18436 | tf_op jit(solution)/shard_map/while
  250.1 16.4 %copy-start.76 = (f32[2,8]{1,0:T(2,128)S(1)}, f32[2,8]{1,0:T(2,128)}, u32[]{:S(2)}) copy-start(f32[2,8]{1,0:T(2,128)} %copy-done.75) | copy-start | bytes 196 | tf_op jit(solution)/shard_map/while
  250.1 16.4 %copy-start.83 = (f32[2]{0:T(128)S(1)}, f32[2]{0:T(128)}, u32[]{:S(2)}) copy-start(f32[2]{0:T(128)} %copy-done.82) | copy-start | bytes 28 | tf_op jit(solution)/shard_map/while
  250.1 16.4 %copy-start.85 = (f32[2]{0:T(128)S(1)}, f32[2]{0:T(128)}, u32[]{:S(2)}) copy-start(f32[2]{0:T(128)} %copy-done.84) | copy-start | bytes 28 | tf_op jit(solution)/shard_map/while
  252.0 14.5 %copy-start.80 = (f32[2]{0:T(128)S(1)}, f32[2]{0:T(128)}, u32[]{:S(2)}) copy-start(f32[2]{0:T(128)} %copy-done.79) | copy-start | bytes 28 | tf_op jit(solution)/shard_map/while
  266.6 13.9 %copy-start.71 = (f32[2,3,256]{2,1,0:T(4,128)}, f32[2,3,256]{2,1,0:T(4,128)S(1)}, u32[]{:S(2)}) copy-start(f32[2,3,256]{2,1,0:T(4,128)S(1)} %get-tuple-element.527) | copy-start | bytes 18436 | tf_op jit(solution)/shard_map/while
  296.6 14.2 %copy-start.70 = (s32[8]{0:T(128)S(1)}, s32[8]{0:T(128)}, u32[]{:S(2)}) copy-start(s32[8]{0:T(128)} %copy-done.69) | copy-start | bytes 100 | tf_op jit(solution)/shard_map/while
  296.6 16.5 %copy-start.72 = (f32[2,3,256]{2,1,0:T(4,128)S(1)}, f32[2,3,256]{2,1,0:T(4,128)}, u32[]{:S(2)}) copy-start(f32[2,3,256]{2,1,0:T(4,128)} %copy-done.71) | copy-start | bytes 18436 | tf_op jit(solution)/shard_map/while
  296.7 16.5 %copy-start.76 = (f32[2,8]{1,0:T(2,128)S(1)}, f32[2,8]{1,0:T(2,128)}, u32[]{:S(2)}) copy-start(f32[2,8]{1,0:T(2,128)} %copy-done.75) | copy-start | bytes 196 | tf_op jit(solution)/shard_map/while
  296.7 16.4 %copy-start.83 = (f32[2]{0:T(128)S(1)}, f32[2]{0:T(128)}, u32[]{:S(2)}) copy-start(f32[2]{0:T(128)} %copy-done.82) | copy-start | bytes 28 | tf_op jit(solution)/shard_map/while
  296.7 16.4 %copy-start.85 = (f32[2]{0:T(128)S(1)}, f32[2]{0:T(128)}, u32[]{:S(2)}) copy-start(f32[2]{0:T(128)} %copy-done.84) | copy-start | bytes 28 | tf_op jit(solution)/shard_map/while
  298.6 14.5 %copy-start.80 = (f32[2]{0:T(128)S(1)}, f32[2]{0:T(128)}, u32[]{:S(2)}) copy-start(f32[2]{0:T(128)} %copy-done.79) | copy-start | bytes 28 | tf_op jit(solution)/shard_map/while
  313.4 197.1 %all-to-all-start.1 = ((f32[128,59,128]{2,1,0:T(8,128)}), f32[128,59,128]{2,1,0:T(8,128)}, u32[]{:S(2)}, u32[]{:S(2)}) async-start(f32[128,59,128]{2,1,0:T(8,128)} %get-tuple-element.121), calls=%async_computation.1 | async-start | bytes 8388608 | tf_op jit(solution)/shard_map/all_to_all | solution.py:229
  324.6 244.6 %copy-start.47 = (f32[59,512]{1,0:T(8,128)S(1)}, f32[59,512]{1,0:T(8,128)}, u32[]{:S(2)}) copy-start(f32[59,512]{1,0:T(8,128)} %param.10) | copy-start | bytes 362500
  324.6 244.6 %copy-start.66 = (f32[59,512]{1,0:T(8,128)S(1)}, f32[59,512]{1,0:T(8,128)}, u32[]{:S(2)}) copy-start(f32[59,512]{1,0:T(8,128)} %param.11) | copy-start | bytes 362500
  324.6 244.6 %copy-start.67 = (f32[59,512]{1,0:T(8,128)S(1)}, f32[59,512]{1,0:T(8,128)}, u32[]{:S(2)}) copy-start(f32[59,512]{1,0:T(8,128)} %param.12) | copy-start | bytes 362500
  324.7 244.6 %copy-start.77 = (f32[59]{0:T(128)S(1)}, f32[59]{0:T(128)}, u32[]{:S(2)}) copy-start(f32[59]{0:T(128)} %constant.298.clone) | copy-start | bytes 712
  324.7 244.6 %all-reduce.26.cloned.1.call-start = ((), (), s32[]{:S(2)}) async-start(), calls=%async_computation.2 | async-start | bytes 262144 | tf_op jit(solution)/shard_map/psum | solution.py:232
  (143 other events, 888.0 us)
Sparse Core Ops, SparseCore 0:
  516.8 52.3 all-reduce.25
where the time goes:
time: 582 us; the launch traced here: 579 us
  waiting for transfers between devices  423 us (73%)
  other arithmetic  54.8 us (9%)
  local copies, waits for them, and re-layouts  32 us (5%)
  starting transfers between devices  31.2 us (5%)
  matrix products  20.5 us (4%)
  between operations  14.2 us (2%)
    all_to_all x1, waiting for transfers between devices, on_device(): lax.all_to_all(cotangent, 'dev', split_axis=0, concat_axis=0, tiled=True)  186 us
    all_to_all x1, waiting for transfers between devices, on_device(): lax.all_to_all(outgoing, 'dev', split_axis=0, concat_axis=0, tiled=True)  185 us
    psum x1, waiting for transfers between devices, on_device(): grad = lax.psum(grad, 'rep')  52.5 us
    all_to_all x1, starting transfers between devices, on_device(): lax.all_to_all(outgoing, 'dev', split_axis=0, concat_axis=0, tiled=True)  20 us
  transfers between devices with their start and end apart: 3, of which 3 were waited for; matrix products, arithmetic and copies ran while one was open for 0% of the time, Pallas kernels for 0%

commit v1 on v0

v1 whole, which is shorter than its diff:
```python
import jax
import jax.numpy as jnp
from jax import lax
from jax.experimental import pallas as pl
from jax.experimental.pallas import tpu as pltpu
from jax.sharding import PartitionSpec as P

BLOCK = 128
PARAMS = 59
FEATS = 9
SLOT = FEATS * BLOCK
TILE = 256
SIDE = 16
LIST = 8
TILES_X = 64
ADAM_STEP = 1000

FOCAL = 1100.0
DEPTH_ZERO = 20.0
BASELINE = 16.0 * DEPTH_ZERO / FOCAL
BLUR = 0.3
SMOOTHING = 0.0001
BETA_ONE = 0.9
BETA_TWO = 0.999
ADAM_EPS = 1e-15
SH_ZERO = 0.28209479177387814
SH_ONE = 0.4886025119029199
SH_TWO = [
    1.0925484305920792,
    -1.0925484305920792,
    0.31539156525252005,
    -1.0925484305920792,
    0.5462742152960396,
]
SH_THREE = [
    -0.5900435899266435,
    2.890611442640554,
    -0.4570457994644658,
    0.3731763325901154,
    -0.4570457994644658,
    1.445305721320277,
    -0.5900435899266435,
]
RATES = [(0, 0.00016), (3, 0.005), (6, 0.001), (10, 0.05), (11, 0.0025), (14, 0.000125)]

VMEM_LIMIT = 40 * 1024 * 1024
SMEM = pltpu.MemorySpace.SMEM
VMEM = pltpu.MemorySpace.VMEM


def sh_basis(unit_x, unit_y, unit_z):
    square_x = unit_x * unit_x
    square_y = unit_y * unit_y
    square_z = unit_z * unit_z
    return [
        SH_ZERO + 0.0 * unit_x,
        -SH_ONE * unit_y,
        SH_ONE * unit_z,
        -SH_ONE * unit_x,
        SH_TWO[0] * unit_x * unit_y,
        SH_TWO[1] * unit_y * unit_z,
        SH_TWO[2] * (2.0 * square_z - square_x - square_y),
        SH_TWO[3] * unit_x * unit_z,
        SH_TWO[4] * (square_x - square_y),
        SH_THREE[0] * unit_y * (3.0 * square_x - square_y),
        SH_THREE[1] * unit_x * unit_y * unit_z,
        SH_THREE[2] * unit_y * (4.0 * square_z - square_x - square_y),
        SH_THREE[3] * unit_z * (2.0 * square_z - 3.0 * square_x - 3.0 * square_y),
        SH_THREE[4] * unit_x * (4.0 * square_z - square_x - square_y),
        SH_THREE[5] * unit_z * (square_x - square_y),
        SH_THREE[6] * unit_x * (square_x - 3.0 * square_y),
    ]


def project(rows, shift, center_x, center_y):
    offset_x = rows[0] - shift
    offset_y = rows[1]
    depth = rows[2]
    inverse = 1.0 / depth
    focal_depth = FOCAL * inverse
    screen_x = focal_depth * offset_x + center_x
    screen_y = focal_depth * offset_y + center_y
    scales = [jnp.exp(rows[3 + index]) for index in range(3)]
    norm = jnp.sqrt(
        rows[6] * rows[6] + rows[7] * rows[7] + rows[8] * rows[8] + rows[9] * rows[9]
    )
    quat_w, quat_x, quat_y, quat_z = [rows[6 + index] / norm for index in range(4)]
    rotation = [
        [
            1.0 - 2.0 * (quat_y * quat_y + quat_z * quat_z),
            2.0 * (quat_x * quat_y - quat_w * quat_z),
            2.0 * (quat_x * quat_z + quat_w * quat_y),
        ],
        [
            2.0 * (quat_x * quat_y + quat_w * quat_z),
            1.0 - 2.0 * (quat_x * quat_x + quat_z * quat_z),
            2.0 * (quat_y * quat_z - quat_w * quat_x),
        ],
        [
            2.0 * (quat_x * quat_z - quat_w * quat_y),
            2.0 * (quat_y * quat_z + quat_w * quat_x),
            1.0 - 2.0 * (quat_x * quat_x + quat_y * quat_y),
        ],
    ]
    slope_x = focal_depth * offset_x * inverse
    slope_y = focal_depth * offset_y * inverse
    first_row = [
        (focal_depth * rotation[0][index] - slope_x * rotation[2][index]) * scales[index]
        for index in range(3)
    ]
    second_row = [
        (focal_depth * rotation[1][index] - slope_y * rotation[2][index]) * scales[index]
        for index in range(3)
    ]
    sigma_xx = (
        first_row[0] * first_row[0]
        + first_row[1] * first_row[1]
        + first_row[2] * first_row[2]
        + BLUR
    )
    sigma_xy = (
        first_row[0] * second_row[0] + first_row[1] * second_row[1] + first_row[2] * second_row[2]
    )
    sigma_yy = (
        second_row[0] * second_row[0]
        + second_row[1] * second_row[1]
        + second_row[2] * second_row[2]
        + BLUR
    )
    determinant = sigma_xx * sigma_yy - sigma_xy * sigma_xy
    distance = jnp.sqrt(offset_x * offset_x + offset_y * offset_y + depth * depth)
    basis = sh_basis(offset_x / distance, offset_y / distance, depth / distance)
    colors = []
    for channel in range(3):
        total = basis[0] * rows[11 + channel]
        for index in range(1, 16):
            total = total + basis[index] * rows[11 + 3 * index + channel]
        colors.append(jnp.maximum(total + 0.5, 0.0))
    return [
        screen_x,
        screen_y,
        sigma_yy / determinant,
        -sigma_xy / determinant,
        sigma_xx / determinant,
        colors[0],
        colors[1],
        colors[2],
    ]


def code_rows(params_ref, blocks_here):
    rows = []
    for row in range(PARAMS):
        parts = [
            params_ref[row : row + 1, block * BLOCK : (block + 1) * BLOCK]
            for block in range(blocks_here)
        ]
        rows.append(jnp.concatenate(parts + parts, axis=0))
    return rows


def code_shift(blocks_here):
    code = lax.broadcasted_iota(jnp.int32, (2 * blocks_here, BLOCK), 0)
    return jnp.where(code >= blocks_here, BASELINE, 0.0).astype(jnp.float32)


def halves(values, pieces):
    out = []
    rest = values
    for index in range(pieces):
        part = rest.astype(jnp.bfloat16)
        out.append(part)
        if index < pieces - 1:
            rest = rest - part.astype(jnp.float32)
    return out


def project_kernel(blocks_here, center_x, center_y, codes_ref, params_ref, out_ref, table_ref):
    rows = code_rows(params_ref, blocks_here)
    shown = project(rows, code_shift(blocks_here), center_x, center_y)
    shown = shown[:5] + [jax.nn.sigmoid(rows[10])] + shown[5:]
    for code in range(2 * blocks_here):
        for feat in range(FEATS):
            table_ref[code, :, feat * BLOCK : (feat + 1) * BLOCK] = shown[feat][code : code + 1]

    def fill(target, carry):
        code = jnp.maximum(codes_ref[target], 0)
        out_ref[target] = table_ref[code]
        return carry

    lax.fori_loop(0, out_ref.shape[0], fill, 0, unroll=8)


def render_kernel(
    tiles_y,
    ids_ref,
    lists_ref,
    slots_ref,
    goal_ref,
    out_ref,
    alpha_ref,
    weight_ref,
    pieces_ref,
    carry_ref,
    color_ref,
    slope_ref,
):
    tiles = ids_ref.shape[0]
    per_view = TILES_X * tiles_y
    f32 = jnp.float32
    lane = lax.broadcasted_iota(jnp.int32, (2 * BLOCK, 2 * BLOCK), 1)
    depth = lax.broadcasted_iota(jnp.int32, (2 * BLOCK, 2 * BLOCK), 0) % BLOCK
    earlier = jnp.where((lane >= BLOCK) | (depth < lane), 1.0, 0.0).astype(jnp.bfloat16)
    later = jnp.where((lane >= BLOCK) | (depth > lane), 1.0, 0.0).astype(jnp.bfloat16)
    ones = jnp.ones((2 * BLOCK, BLOCK), jnp.bfloat16)
    column = lax.broadcasted_iota(jnp.int32, (SIDE, BLOCK), 0).astype(f32) - (SIDE / 2 - 0.5)

    out_ref[...] = jnp.zeros_like(out_ref)
    carry_ref[...] = jnp.zeros_like(carry_ref)
    color_ref[...] = jnp.zeros_like(color_ref)

    def feature(slot, index):
        return slots_ref[slot, :, index * BLOCK : (index + 1) * BLOCK]

    def center(tile):
        within = lax.rem(ids_ref[tile], per_view)
        middle_x = (lax.rem(within, TILES_X) * SIDE + SIDE // 2).astype(f32)
        middle_y = (lax.div(within, TILES_X) * SIDE + SIDE // 2).astype(f32)
        return middle_x, middle_y

    def row_of(index):
        return slice(index * SIDE, (index + 1) * SIDE)

    def forward(layer, carry):
        for tile in range(tiles):
            entry = lists_ref[tile * LIST + layer]
            slot = jnp.maximum(entry, 0)
            live = jnp.where(entry >= 0, 1.0, 0.0).astype(f32)
            middle_x, middle_y = center(tile)
            delta_x = column - (feature(slot, 0) - middle_x)
            place_y = feature(slot, 1) - middle_y
            half_x = (-0.5 * feature(slot, 2)) * delta_x * delta_x
            cross = -feature(slot, 3) * delta_x
            half_y = jnp.broadcast_to(-0.5 * feature(slot, 4), (SIDE, BLOCK))
            opacity = jnp.broadcast_to(feature(slot, 5) * live, (SIDE, BLOCK))
            place_y = jnp.broadcast_to(place_y, (SIDE, BLOCK))
            for row in range(SIDE):
                delta_y = (row - (SIDE / 2 - 0.5)) - place_y
                power = half_x + delta_y * (cross + half_y * delta_y)
                alpha = opacity * jnp.exp(power)
                alpha_ref[tile, layer, row_of(row)] = alpha
                high, low = halves(jnp.log(1.0 - alpha), 2)
                start = tile * TILE + row * SIDE
                pieces_ref[start : start + SIDE, :BLOCK] = high
                pieces_ref[start : start + SIDE, BLOCK:] = low
        sums = jnp.dot(pieces_ref[...], earlier, preferred_element_type=f32)
        for tile in range(tiles):
            slot = jnp.maximum(lists_ref[tile * LIST + layer], 0)
            shades = [
                jnp.broadcast_to(feature(slot, 6 + channel), (SIDE, BLOCK)) for channel in range(3)
            ]
            for row in range(SIDE):
                start = tile * TILE + row * SIDE
                before = carry_ref[tile, row_of(row)]
                weight = alpha_ref[tile, layer, row_of(row)] * jnp.exp(
                    sums[start : start + SIDE, :BLOCK] + before
                )
                weight_ref[tile, layer, row_of(row)] = weight
                carry_ref[tile, row_of(row)] = before + sums[start : start + SIDE, BLOCK:]
                for channel in range(3):
                    color_ref[tile, channel, row_of(row)] += weight * shades[channel]
        return carry

    lax.fori_loop(0, LIST, forward, 0)

    for tile in range(tiles):
        goals = jnp.concatenate([goal_ref[tile], jnp.zeros((5, TILE), f32)], axis=0).T
        for channel in range(3):
            high, low = halves(color_ref[tile, channel], 2)
            color = jnp.dot(
                jnp.concatenate([high, low], axis=1), ones, preferred_element_type=f32
            )
            error = color - goals[:, channel : channel + 1]
            slope_ref[tile, channel] = error * lax.rsqrt(error * error + SMOOTHING) * (1.0 / 3.0)
    carry_ref[...] = jnp.zeros_like(carry_ref)

    def backward(step, carry):
        layer = LIST - 1 - step
        color_grads = []
        for tile in range(tiles):
            slot = jnp.maximum(lists_ref[tile * LIST + layer], 0)
            shades = [
                jnp.broadcast_to(feature(slot, 6 + channel), (SIDE, BLOCK)) for channel in range(3)
            ]
            grads = [jnp.zeros((SIDE, BLOCK), f32) for _ in range(3)]
            for row in range(SIDE):
                weight = weight_ref[tile, layer, row_of(row)]
                pulled = [weight * slope_ref[tile, channel, row_of(row)] for channel in range(3)]
                grads = [grads[channel] + pulled[channel] for channel in range(3)]
                gain = (
                    pulled[0] * shades[0] + pulled[1] * shades[1] + pulled[2] * shades[2]
                )
                weight_ref[tile, layer, row_of(row)] = gain
                high, low = halves(gain, 2)
                start = tile * TILE + row * SIDE
                pieces_ref[start : start + SIDE, :BLOCK] = high
                pieces_ref[start : start + SIDE, BLOCK:] = low
            color_grads.append([jnp.sum(grad, axis=0, keepdims=True) for grad in grads])
        sums = jnp.dot(pieces_ref[...], later, preferred_element_type=f32)
        for tile in range(tiles):
            entry = lists_ref[tile * LIST + layer]
            slot = jnp.maximum(entry, 0)
            middle_x, middle_y = center(tile)
            delta_x = column - (feature(slot, 0) - middle_x)
            place_y = jnp.broadcast_to(feature(slot, 1) - middle_y, (SIDE, BLOCK))
            flat = jnp.zeros((SIDE, BLOCK), f32)
            tilt = jnp.zeros((SIDE, BLOCK), f32)
            bend = jnp.zeros((SIDE, BLOCK), f32)
            for row in range(SIDE):
                start = tile * TILE + row * SIDE
                alpha = alpha_ref[tile, layer, row_of(row)]
                after = carry_ref[tile, row_of(row)]
                behind = sums[start : start + SIDE, :BLOCK] + after
                carry_ref[tile, row_of(row)] = after + sums[start : start + SIDE, BLOCK:]
                power_grad = weight_ref[tile, layer, row_of(row)] - behind * (
                    alpha / (1.0 - alpha)
                )
                delta_y = (row - (SIDE / 2 - 0.5)) - place_y
                turned = power_grad * delta_y
                flat += power_grad
                tilt += turned
                bend += turned * delta_y

            def total(values):
                return jnp.sum(values, axis=0, keepdims=True)

            sum_x = total(flat * delta_x)
            sum_y = total(tilt)
            conic_a, conic_b, conic_c = feature(slot, 2), feature(slot, 3), feature(slot, 4)
            results = [
                conic_a * sum_x + conic_b * sum_y,
                conic_b * sum_x + conic_c * sum_y,
                -0.5 * total(flat * delta_x * delta_x),
                -total(tilt * delta_x),
                -0.5 * total(bend),
                total(flat),
            ] + color_grads[tile]

            @pl.when(entry >= 0)
            def _():
                for index in range(FEATS):
                    out_ref[slot, :, index * BLOCK : (index + 1) * BLOCK] = results[index]

        return carry

    lax.fori_loop(0, LIST, backward, 0)


def collect_kernel(keys_ref, slots_ref, out_ref):
    count, width = out_ref.shape[0], slots_ref.shape[0]
    wanted = lax.broadcasted_iota(jnp.int32, (count, width), 0)
    picker = jnp.where(keys_ref[...] == wanted, 1.0, 0.0).astype(jnp.bfloat16)
    total = jnp.zeros(out_ref.shape, jnp.float32)
    for piece in halves(slots_ref[...], 3):
        total += jnp.dot(picker, piece, preferred_element_type=jnp.float32)
    out_ref[...] = total


def update_kernel(
    blocks_here,
    center_x,
    center_y,
    cot_ref,
    params_ref,
    adam_m_ref,
    adam_v_ref,
    new_params_ref,
    new_m_ref,
    new_v_ref,
    grad_ref,
):
    codes = 2 * blocks_here
    rows = code_rows(params_ref, blocks_here)
    shift = code_shift(blocks_here)
    cots = [cot_ref[codes * feat : codes * (feat + 1)] for feat in range(FEATS)]
    used = rows[:10] + rows[11:]

    def shown_of(values):
        return project(values[:10] + [None] + values[10:], shift, center_x, center_y)

    _, pull = jax.vjp(shown_of, used)
    grads = pull(cots[:5] + cots[6:])[0]
    logit_grad = cots[5] * (1.0 - jax.nn.sigmoid(rows[10]))
    grads = grads[:10] + [logit_grad] + grads[10:]
    for row in range(PARAMS):
        both = grads[row][:blocks_here] + grads[row][blocks_here:]
        for block in range(blocks_here):
            grad_ref[row : row + 1, block * BLOCK : (block + 1) * BLOCK] = both[block : block + 1]
    grad = grad_ref[...]
    new_m = BETA_ONE * adam_m_ref[...] + (1.0 - BETA_ONE) * grad
    new_v = BETA_TWO * adam_v_ref[...] + (1.0 - BETA_TWO) * grad * grad
    m_hat = new_m * (1.0 / (1.0 - BETA_ONE**ADAM_STEP))
    v_hat = new_v * (1.0 / (1.0 - BETA_TWO**ADAM_STEP))
    row = lax.broadcasted_iota(jnp.int32, grad.shape, 0)
    rates = jnp.full(grad.shape, RATES[0][1], jnp.float32)
    for first, rate in RATES[1:]:
        rates = jnp.where(row >= first, jnp.float32(rate), rates)
    new_params_ref[...] = params_ref[...] - rates * m_hat / (jnp.sqrt(v_hat) + ADAM_EPS)
    new_m_ref[...] = new_m
    new_v_ref[...] = new_v


def vmem(count):
    return [pl.BlockSpec(memory_space=VMEM)] * count


def smem(count):
    return [pl.BlockSpec(memory_space=SMEM)] * count


def on_device(params, adam_m, adam_v, target, tile_ids, send_blocks, tile_lists):
    dev_count = lax.axis_size("dev")
    g_local = params.shape[1]
    blocks_here = g_local // BLOCK
    codes = 2 * blocks_here
    tiles_y = dev_count * blocks_here // TILES_X
    center_x = 8.0 * TILES_X
    center_y = 8.0 * tiles_y
    tiles = tile_ids.shape[2]
    f32 = jnp.float32
    limit = pltpu.CompilerParams(vmem_limit_bytes=VMEM_LIMIT)
    provided = send_blocks.reshape(-1)
    slot_shape = jax.ShapeDtypeStruct((dev_count, 1, SLOT), f32)

    outgoing = pl.pallas_call(
        lambda *refs: project_kernel(blocks_here, center_x, center_y, *refs),
        out_shape=slot_shape,
        in_specs=smem(1) + vmem(1),
        out_specs=vmem(1)[0],
        scratch_shapes=[pltpu.VMEM((codes, 1, SLOT), f32)],
        compiler_params=limit,
        name="project",
    )(provided, params)
    incoming = lax.all_to_all(outgoing, "dev", split_axis=0, concat_axis=0, tiled=True)
    pairs = pltpu.VMEM((tiles, LIST, TILE, BLOCK), f32)
    cotangent = pl.pallas_call(
        lambda *refs: render_kernel(tiles_y, *refs),
        out_shape=slot_shape,
        in_specs=smem(2) + vmem(2),
        out_specs=vmem(1)[0],
        scratch_shapes=[
            pairs,
            pairs,
            pltpu.VMEM((tiles * TILE, 2 * BLOCK), jnp.bfloat16),
            pltpu.VMEM((tiles, TILE, BLOCK), f32),
            pltpu.VMEM((tiles, 3, TILE, BLOCK), f32),
            pltpu.VMEM((tiles, 3, TILE, BLOCK), f32),
        ],
        compiler_params=limit,
        name="render",
    )(tile_ids.reshape(-1), tile_lists.reshape(-1), incoming, target.reshape(target.shape[2:]))
    returned = lax.all_to_all(cotangent, "dev", split_axis=0, concat_axis=0, tiled=True)
    order = jnp.arange(FEATS, dtype=jnp.int32) * codes
    keys = jnp.where(provided[:, None] >= 0, provided[:, None] + order[None, :], -1)
    per_code = pl.pallas_call(
        collect_kernel,
        out_shape=jax.ShapeDtypeStruct((FEATS * codes, BLOCK), f32),
        in_specs=vmem(2),
        out_specs=vmem(1)[0],
        compiler_params=limit,
        name="collect",
    )(keys.reshape(1, dev_count * FEATS), returned.reshape(dev_count * FEATS, BLOCK))
    per_code = lax.psum(per_code, "rep")
    shape = jax.ShapeDtypeStruct(params.shape, f32)
    return pl.pallas_call(
        lambda *refs: update_kernel(blocks_here, center_x, center_y, *refs),
        out_shape=(shape,) * 4,
        in_specs=vmem(4),
        out_specs=tuple(vmem(4)),
        compiler_params=limit,
        name="update",
    )(per_code, params, adam_m, adam_v)


def solution(mesh):
    placed = (
        P(None, "dev"),
        P(None, "dev"),
        P(None, "dev"),
        P("rep", "dev", None, None, None),
        P("rep", "dev", None),
        P("rep", "dev", None, None),
        P("rep", "dev", None, None),
    )
    return jax.shard_map(
        on_device,
        mesh=mesh,
        in_specs=placed,
        out_specs=(P(None, "dev"), P(None, "dev"), P(None, "dev"), P(None, "dev")),
        check_vma=False,
    )
```

time: 582 us -> 129 us (0.22)
  waiting for transfers between devices: 423 us -> 70.1 us
  other arithmetic: 54.8 us -> 0.11 us
  local copies, waits for them, and re-layouts: 32 us -> 3.18 us
  matrix products: 20.5 us -> 0 us
  blocking collectives: 0 us -> 17.6 us
  between operations: 14.2 us -> 0.75 us
  Pallas kernels: 0 us -> 10.3 us
    all_to_all x1, waiting for transfers between devices: 186 us -> 35.3 us  [on_device(): lax.all_to_all(cotangent, 'dev', split_axis=0, concat_axis=0, tiled=True)]
    all_to_all x1, waiting for transfers between devices: 185 us -> 34.8 us  [on_device(): lax.all_to_all(outgoing, 'dev', split_axis=0, concat_axis=0, tiled=True)]
    psum x1 -> x0, waiting for transfers between devices: 52.5 us -> none  [on_device(): grad = lax.psum(grad, 'rep')]
    add_any x24 -> x0, other arithmetic: 22.2 us -> none  [the longest x2 3.59 us: project(): inverse = 1.0 / depth]
    dot_general x11 -> x0, matrix products: 20.5 us -> none  [the longest x6 8.8 us: render_loss(): jnp.einsum('ck,pk->cp', features[6:9], weight, precision=lax.Precision.HI...]
    psum x0 -> x1, blocking collectives: none -> 17.6 us  [on_device(): per_code = lax.psum(per_code, 'rep')]
    reduce_sum x12 -> x0, other arithmetic: 10.4 us -> none  [the longest x2 3.62 us: render_loss(): features[3] * delta_x * delta_y]
    pallas_call x0 -> x4, Pallas kernels: none -> 10.3 us  [the longest x1 7.16 us: on_device(): pl.pallas_call(lambda *refs: render_kernel(tiles_y, *refs), out_shape=slo...]
  transfers between devices with their start and end apart: 3 -> 2, of which waited for: 3 -> 2; matrix products, arithmetic and copies ran while one was open for 0% -> 0% of each run, Pallas kernels for 0% -> 0%
where the time goes in v1:
time: 129 us
  waiting for transfers between devices  70.1 us (54%)
  starting transfers between devices  26.6 us (21%)
  blocking collectives  17.6 us (14%)
  Pallas kernels  10.3 us (8%)
  local copies, waits for them, and re-layouts  3.18 us (2%)
    all_to_all x1, waiting for transfers between devices, on_device(): lax.all_to_all(cotangent, 'dev', split_axis=0, concat_axis=0, tiled=True)  35.3 us
    all_to_all x1, waiting for transfers between devices, on_device(): lax.all_to_all(outgoing, 'dev', split_axis=0, concat_axis=0, tiled=True)  34.8 us
    all_to_all x1, starting transfers between devices, on_device(): lax.all_to_all(outgoing, 'dev', split_axis=0, concat_axis=0, tiled=True)  19.5 us
    psum x1, blocking collectives, on_device(): per_code = lax.psum(per_code, 'rep')  17.6 us
    pallas_call x1, Pallas kernels, on_device(): pl.pallas_call(lambda *refs: render_kernel(tiles_y, *refs), out_shape=slo...  7.16 us
    all_to_all x1, starting transfers between devices, on_device(): lax.all_to_all(cotangent, 'dev', split_axis=0, concat_axis=0, tiled=True)  7.1 us
    unnamed x17, local copies, waits for them, and re-layouts  2.89 us
  transfers between devices with their start and end apart: 2, of which 2 were waited for; matrix products, arithmetic and copies ran while one was open for 0% of the time, Pallas kernels for 0%

profile of v1, /device:TPU:6, one launch (start us, length us, event | category | flops | bytes accessed | tf_op | source)
XLA Modules:
  0.0 128.6 jit_solution(2302261525332583035)
XLA Ops:
  0.6 0.0 copy-start.4
  0.6 0.6 copy-done.4
  1.3 0.0 copy-start
  1.3 0.9 copy-done
  2.2 1.8 %project.1 = f32[128,1,1152]{2,1,0:T(1,128)} custom-call(s32[128]{0:T(128)S(1)} %bitcast.9, f32[59,512]{1,0:T(8,128)S(1)} %copy-done), custom_call_target="tpu_custom_call" | custom-call | tf_op jit(solution)/shard_map/project/pallas_call | solution.py:435
  4.0 0.0 copy-start.6
  4.0 19.5 %all-to-all-start = ((f32[128,1,1152]{2,1,0:T(1,128)}), f32[128,1,1152]{2,1,0:T(1,128)S(1)}, u32[]{:S(2)}, u32[]{:S(2)}) async-start(f32[128,1,1152]{2,1,0:T(1,128)} %project.1), calls=%async_computation | async-start | bytes 1179648 | tf_op jit(solution)/shard_map/all_to_all | solution.py:444
  23.5 0.0 copy-done.6
  23.5 0.0 copy-start.7
  23.5 0.7 copy-done.7
  24.2 0.1 reshape.71.refs_1_
  24.3 34.8 %all-to-all-done.refs_2_ = f32[128,1,1152]{2,1,0:T(1,128)S(1)} async-done(((f32[128,1,1152]{2,1,0:T(1,128)}), f32[128,1,1152]{2,1,0:T(1,128)S(1)}, u32[]{:S(2)}, u32[]{:S(2)}) %all-to-all-start) | async-done | bytes 589856 | tf_op jit(solution)/shard_map/all_to_all | solution.py:444
  59.1 0.7 copy-done.5
  59.7 7.2 %render.1 = f32[128,1,1152]{2,1,0:T(1,128)} custom-call(s32[2]{0:T(128)S(1)} %bitcast.11, s32[16]{0:T(128)S(1)} %reshape.71.refs_1_, f32[128,1,1152]{2,1,0:T(1,128)S(1)} %all-to-all-done.refs_2_, f32[2,3,256]{2,1,0:T(4,128)S(1)} %bitcast.8), custom_call_target="tpu_custom_call" | custom-call | tf_op jit(solution)/shard_map/render/pallas_call | solution.py:446
  66.9 7.1 %all-to-all-start.1 = ((f32[128,1,1152]{2,1,0:T(1,128)}), f32[128,1,1152]{2,1,0:T(1,128)S(1)}, u32[]{:S(2)}, u32[]{:S(2)}) async-start(f32[128,1,1152]{2,1,0:T(1,128)} %render.1), calls=%async_computation.1 | async-start | bytes 1179648 | tf_op jit(solution)/shard_map/all_to_all | solution.py:462
  74.0 0.1 add_select_fusion
  74.1 0.2 select_n.15.keys_ref
  74.3 35.3 %all-to-all-done.1 = f32[128,1,1152]{2,1,0:T(1,128)S(1)} async-done(((f32[128,1,1152]{2,1,0:T(1,128)}), f32[128,1,1152]{2,1,0:T(1,128)S(1)}, u32[]{:S(2)}, u32[]{:S(2)}) %all-to-all-start.1) | async-done | bytes 589856 | tf_op jit(solution)/shard_map/all_to_all | solution.py:462
  109.6 0.3 collect.1
  110.0 17.6 %psum.7.refs_0_ = f32[72,128]{1,0:T(8,128)S(1)} all-reduce(f32[72,128]{1,0:T(8,128)S(1)} %collect.1), channel_id=1, replica_groups=mesh['rep'=4,'dev'=128] {'rep'}, use_global_device_ids=true, to_apply=%region_0.1 | all-reduce | flops 9216 | bytes 73728 | tf_op jit(solution)/shard_map/psum | solution.py:473
  127.6 0.0 copy-done.1
  127.6 0.0 copy-done.2
  127.6 0.0 copy-done.3
  127.6 1.1 update.1
  (7 shorter events, 0.0 us)
Async XLA Ops:
  0.6 0.7 copy-start.4
  1.3 0.9 copy-start
  4.0 19.5 %copy-start.6 = (f32[1,1,2,3,256]{4,2,3,1,0:T(2,128)S(1)}, f32[1,1,2,3,256]{4,2,3,1,0:T(2,128)}, u32[]{:S(2)}) copy-start(f32[1,1,2,3,256]{4,2,3,1,0:T(2,128)} %param.10) | copy-start | bytes 18436
  4.0 55.1 %all-to-all-start = ((f32[128,1,1152]{2,1,0:T(1,128)}), f32[128,1,1152]{2,1,0:T(1,128)S(1)}, u32[]{:S(2)}, u32[]{:S(2)}) async-start(f32[128,1,1152]{2,1,0:T(1,128)} %project.1), calls=%async_computation | async-start | bytes 1179648 | tf_op jit(solution)/shard_map/all_to_all | solution.py:444
  23.5 0.7 copy-start.7
  59.1 0.7 copy-start.5
  66.9 42.7 %all-to-all-start.1 = ((f32[128,1,1152]{2,1,0:T(1,128)}), f32[128,1,1152]{2,1,0:T(1,128)S(1)}, u32[]{:S(2)}, u32[]{:S(2)}) async-start(f32[128,1,1152]{2,1,0:T(1,128)} %render.1), calls=%async_computation.1 | async-start | bytes 1179648 | tf_op jit(solution)/shard_map/all_to_all | solution.py:462
  109.6 18.0 %copy-start.1 = (f32[59,512]{1,0:T(8,128)S(1)}, f32[59,512]{1,0:T(8,128)}, u32[]{:S(2)}) copy-start(f32[59,512]{1,0:T(8,128)} %refs_1_.3) | copy-start | bytes 362500
  109.6 18.0 %copy-start.2 = (f32[59,512]{1,0:T(8,128)S(1)}, f32[59,512]{1,0:T(8,128)}, u32[]{:S(2)}) copy-start(f32[59,512]{1,0:T(8,128)} %refs_2_.1) | copy-start | bytes 362500
  109.6 18.0 %copy-start.3 = (f32[59,512]{1,0:T(8,128)S(1)}, f32[59,512]{1,0:T(8,128)}, u32[]{:S(2)}) copy-start(f32[59,512]{1,0:T(8,128)} %refs_3_.1) | copy-start | bytes 362500

commit v2 on v1

--- a/solution.py
+++ b/solution.py
@@ -175,26 +175,36 @@
     return out
 
 
-def project_kernel(blocks_here, center_x, center_y, codes_ref, params_ref, out_ref, table_ref):
+def project_kernel(
+    blocks_here, center_x, center_y, codes_hbm, params_hbm, out_ref, codes_ref, params_ref, table_ref, sems
+):
+    copies = [
+        pltpu.make_async_copy(params_hbm, params_ref, sems.at[0]),
+        pltpu.make_async_copy(codes_hbm, codes_ref, sems.at[1]),
+    ]
+    for copy in copies:
+        copy.start()
+    copies[0].wait()
     rows = code_rows(params_ref, blocks_here)
     shown = project(rows, code_shift(blocks_here), center_x, center_y)
     shown = shown[:5] + [jax.nn.sigmoid(rows[10])] + shown[5:]
     for code in range(2 * blocks_here):
         for feat in range(FEATS):
-            table_ref[code, :, feat * BLOCK : (feat + 1) * BLOCK] = shown[feat][code : code + 1]
+            table_ref[code, feat : feat + 1] = shown[feat][code : code + 1]
+    copies[1].wait()
 
     def fill(target, carry):
         code = jnp.maximum(codes_ref[target], 0)
-        out_ref[target] = table_ref[code]
+        out_ref[pl.ds(target * FEATS, 8)] = table_ref[code, 0:8]
+        out_ref[pl.ds(target * FEATS + 8, 1)] = table_ref[code, 8:9]
         return carry
 
-    lax.fori_loop(0, out_ref.shape[0], fill, 0, unroll=8)
+    lax.fori_loop(0, out_ref.shape[0] // FEATS, fill, 0, unroll=8)
 
 
 def render_kernel(
     tiles_y,
-    ids_ref,
-    lists_ref,
+    scalars_ref,
     slots_ref,
     goal_ref,
     out_ref,
@@ -205,73 +215,95 @@
     color_ref,
     slope_ref,
 ):
-    tiles = ids_ref.shape[0]
+    tiles = goal_ref.shape[0]
     per_view = TILES_X * tiles_y
     f32 = jnp.float32
+    half = SIDE // 2
     lane = lax.broadcasted_iota(jnp.int32, (2 * BLOCK, 2 * BLOCK), 1)
     depth = lax.broadcasted_iota(jnp.int32, (2 * BLOCK, 2 * BLOCK), 0) % BLOCK
     earlier = jnp.where((lane >= BLOCK) | (depth < lane), 1.0, 0.0).astype(jnp.bfloat16)
     later = jnp.where((lane >= BLOCK) | (depth > lane), 1.0, 0.0).astype(jnp.bfloat16)
     ones = jnp.ones((2 * BLOCK, BLOCK), jnp.bfloat16)
-    column = lax.broadcasted_iota(jnp.int32, (SIDE, BLOCK), 0).astype(f32) - (SIDE / 2 - 0.5)
+    column = lax.broadcasted_iota(jnp.int32, (half, BLOCK), 0).astype(f32) - (SIDE / 2 - 0.5)
 
     out_ref[...] = jnp.zeros_like(out_ref)
-    carry_ref[...] = jnp.zeros_like(carry_ref)
-    color_ref[...] = jnp.zeros_like(color_ref)
+
+    def entry_of(tile, layer):
+        return scalars_ref[tiles + tile * LIST + layer]
 
     def feature(slot, index):
-        return slots_ref[slot, :, index * BLOCK : (index + 1) * BLOCK]
+        return slots_ref[pl.ds(slot * FEATS + index, 1)]
+
+    def wide(row):
+        return jnp.broadcast_to(row, (half, BLOCK))
 
     def center(tile):
-        within = lax.rem(ids_ref[tile], per_view)
-        middle_x = (lax.rem(within, TILES_X) * SIDE + SIDE // 2).astype(f32)
-        middle_y = (lax.div(within, TILES_X) * SIDE + SIDE // 2).astype(f32)
+        within = lax.rem(scalars_ref[tile], per_view)
+        middle_x = (lax.rem(within, TILES_X) * SIDE + half).astype(f32)
+        middle_y = (lax.div(within, TILES_X) * SIDE + half).astype(f32)
         return middle_x, middle_y
 
-    def row_of(index):
-        return slice(index * SIDE, (index + 1) * SIDE)
+    def row_of(index, part):
+        start = index * SIDE + part * half
+        return slice(start, start + half)
+
+    def offsets(tile, slot):
+        middle_x, middle_y = center(tile)
+        place_x = wide(feature(slot, 0) - middle_x)
+        place_y = wide(feature(slot, 1) - middle_y)
+        return [column + part * half - place_x for part in range(2)], place_y
+
+    def split_row(tile, row, parts):
+        pairs = [halves(part, 2) for part in parts]
+        start = tile * TILE + row * SIDE
+        for side in range(2):
+            both = jnp.concatenate([pair[side] for pair in pairs], axis=0)
+            pieces_ref[start : start + SIDE, side * BLOCK : (side + 1) * BLOCK] = both
+
+    def add_up(matrix):
+        return jnp.dot(pieces_ref[...], matrix, preferred_element_type=f32)
 
     def forward(layer, carry):
         for tile in range(tiles):
-            entry = lists_ref[tile * LIST + layer]
+            entry = entry_of(tile, layer)
             slot = jnp.maximum(entry, 0)
             live = jnp.where(entry >= 0, 1.0, 0.0).astype(f32)
-            middle_x, middle_y = center(tile)
-            delta_x = column - (feature(slot, 0) - middle_x)
-            place_y = feature(slot, 1) - middle_y
-            half_x = (-0.5 * feature(slot, 2)) * delta_x * delta_x
-            cross = -feature(slot, 3) * delta_x
-            half_y = jnp.broadcast_to(-0.5 * feature(slot, 4), (SIDE, BLOCK))
-            opacity = jnp.broadcast_to(feature(slot, 5) * live, (SIDE, BLOCK))
-            place_y = jnp.broadcast_to(place_y, (SIDE, BLOCK))
+            delta_x, place_y = offsets(tile, slot)
+            half_x = [wide(-0.5 * feature(slot, 2)) * delta * delta for delta in delta_x]
+            cross = [wide(-feature(slot, 3)) * delta for delta in delta_x]
+            half_y = wide(-0.5 * feature(slot, 4))
+            opacity = wide(feature(slot, 5) * live)
             for row in range(SIDE):
                 delta_y = (row - (SIDE / 2 - 0.5)) - place_y
-                power = half_x + delta_y * (cross + half_y * delta_y)
-                alpha = opacity * jnp.exp(power)
-                alpha_ref[tile, layer, row_of(row)] = alpha
-                high, low = halves(jnp.log(1.0 - alpha), 2)
-                start = tile * TILE + row * SIDE
-                pieces_ref[start : start + SIDE, :BLOCK] = high
-                pieces_ref[start : start + SIDE, BLOCK:] = low
-        sums = jnp.dot(pieces_ref[...], earlier, preferred_element_type=f32)
+                scaled_y = half_y * delta_y
+                logs = []
+                for part in range(2):
+                    power = half_x[part] + delta_y * (cross[part] + scaled_y)
+                    alpha = opacity * jnp.exp(power)
+                    alpha_ref[tile, layer, row_of(row, part)] = alpha
+                    logs.append(jnp.log(1.0 - alpha))
+                split_row(tile, row, logs)
+        sums = add_up(earlier)
         for tile in range(tiles):
-            slot = jnp.maximum(lists_ref[tile * LIST + layer], 0)
-            shades = [
-                jnp.broadcast_to(feature(slot, 6 + channel), (SIDE, BLOCK)) for channel in range(3)
-            ]
+            slot = jnp.maximum(entry_of(tile, layer), 0)
+            shades = [wide(feature(slot, 6 + channel)) for channel in range(3)]
             for row in range(SIDE):
-                start = tile * TILE + row * SIDE
-                before = carry_ref[tile, row_of(row)]
-                weight = alpha_ref[tile, layer, row_of(row)] * jnp.exp(
-                    sums[start : start + SIDE, :BLOCK] + before
-                )
-                weight_ref[tile, layer, row_of(row)] = weight
-                carry_ref[tile, row_of(row)] = before + sums[start : start + SIDE, BLOCK:]
-                for channel in range(3):
-                    color_ref[tile, channel, row_of(row)] += weight * shades[channel]
+                for part in range(2):
+                    where = row_of(row, part)
+                    start = tile * TILE + where.start
+                    before = carry_ref[tile, where]
+                    weight = alpha_ref[tile, layer, where] * jnp.exp(
+                        sums[start : start + half, :BLOCK] + before
+                    )
+                    weight_ref[tile, layer, where] = weight
+                    carry_ref[tile, where] = before + sums[start : start + half, BLOCK:]
+                    for channel in range(3):
+                        color_ref[tile, channel, where] += weight * shades[channel]
         return carry
 
-    lax.fori_loop(0, LIST, forward, 0)
+    color_ref[...] = jnp.zeros_like(color_ref)
+    carry_ref[...] = jnp.zeros_like(carry_ref)
+    lax.fori_loop(0, LIST, forward, 0, unroll=8)
 
     for tile in range(tiles):
         goals = jnp.concatenate([goal_ref[tile], jnp.zeros((5, TILE), f32)], axis=0).T
@@ -284,76 +316,66 @@
             slope_ref[tile, channel] = error * lax.rsqrt(error * error + SMOOTHING) * (1.0 / 3.0)
     carry_ref[...] = jnp.zeros_like(carry_ref)
 
+    def total(values):
+        return jnp.sum(values, axis=0, keepdims=True)
+
     def backward(step, carry):
         layer = LIST - 1 - step
         color_grads = []
         for tile in range(tiles):
-            slot = jnp.maximum(lists_ref[tile * LIST + layer], 0)
-            shades = [
-                jnp.broadcast_to(feature(slot, 6 + channel), (SIDE, BLOCK)) for channel in range(3)
-            ]
-            grads = [jnp.zeros((SIDE, BLOCK), f32) for _ in range(3)]
+            slot = jnp.maximum(entry_of(tile, layer), 0)
+            shades = [wide(feature(slot, 6 + channel)) for channel in range(3)]
+            grads = [jnp.zeros((half, BLOCK), f32) for _ in range(3)]
             for row in range(SIDE):
-                weight = weight_ref[tile, layer, row_of(row)]
-                pulled = [weight * slope_ref[tile, channel, row_of(row)] for channel in range(3)]
-                grads = [grads[channel] + pulled[channel] for channel in range(3)]
-                gain = (
-                    pulled[0] * shades[0] + pulled[1] * shades[1] + pulled[2] * shades[2]
-                )
-                weight_ref[tile, layer, row_of(row)] = gain
-                high, low = halves(gain, 2)
-                start = tile * TILE + row * SIDE
-                pieces_ref[start : start + SIDE, :BLOCK] = high
-                pieces_ref[start : start + SIDE, BLOCK:] = low
-            color_grads.append([jnp.sum(grad, axis=0, keepdims=True) for grad in grads])
-        sums = jnp.dot(pieces_ref[...], later, preferred_element_type=f32)
+                parts = []
+                for part in range(2):
+                    where = row_of(row, part)
+                    weight = weight_ref[tile, layer, where]
+                    pulled = [weight * slope_ref[tile, channel, where] for channel in range(3)]
+                    grads = [grads[channel] + pulled[channel] for channel in range(3)]
+                    gain = pulled[0] * shades[0] + pulled[1] * shades[1] + pulled[2] * shades[2]
+                    weight_ref[tile, layer, where] = gain
+                    parts.append(gain)
+                split_row(tile, row, parts)
+            color_grads.append([total(grad) for grad in grads])
+        sums = add_up(later)
         for tile in range(tiles):
-            entry = lists_ref[tile * LIST + layer]
-            slot = jnp.maximum(entry, 0)
-            middle_x, middle_y = center(tile)
-            delta_x = column - (feature(slot, 0) - middle_x)
-            place_y = jnp.broadcast_to(feature(slot, 1) - middle_y, (SIDE, BLOCK))
-            flat = jnp.zeros((SIDE, BLOCK), f32)
-            tilt = jnp.zeros((SIDE, BLOCK), f32)
-            bend = jnp.zeros((SIDE, BLOCK), f32)
+            slot = jnp.maximum(entry_of(tile, layer), 0)
+            delta_x, place_y = offsets(tile, slot)
+            flat = [jnp.zeros((half, BLOCK), f32) for _ in range(2)]
+            tilt = [jnp.zeros((half, BLOCK), f32) for _ in range(2)]
+            bend = jnp.zeros((half, BLOCK), f32)
             for row in range(SIDE):
-                start = tile * TILE + row * SIDE
-                alpha = alpha_ref[tile, layer, row_of(row)]
-                after = carry_ref[tile, row_of(row)]
-                behind = sums[start : start + SIDE, :BLOCK] + after
-                carry_ref[tile, row_of(row)] = after + sums[start : start + SIDE, BLOCK:]
-                power_grad = weight_ref[tile, layer, row_of(row)] - behind * (
-                    alpha / (1.0 - alpha)
-                )
                 delta_y = (row - (SIDE / 2 - 0.5)) - place_y
-                turned = power_grad * delta_y
-                flat += power_grad
-                tilt += turned
-                bend += turned * delta_y
-
-            def total(values):
-                return jnp.sum(values, axis=0, keepdims=True)
-
-            sum_x = total(flat * delta_x)
-            sum_y = total(tilt)
+                for part in range(2):
+                    where = row_of(row, part)
+                    start = tile * TILE + where.start
+                    alpha = alpha_ref[tile, layer, where]
+                    after = carry_ref[tile, where]
+                    behind = sums[start : start + half, :BLOCK] + after
+                    carry_ref[tile, where] = after + sums[start : start + half, BLOCK:]
+                    power_grad = weight_ref[tile, layer, where] - behind * (alpha / (1.0 - alpha))
+                    turned = power_grad * delta_y
+                    flat[part] += power_grad
+                    tilt[part] += turned
+                    bend += turned * delta_y
+            leaned = [flat[part] * delta_x[part] for part in range(2)]
+            sum_x = total(leaned[0] + leaned[1])
+            sum_y = total(tilt[0] + tilt[1])
             conic_a, conic_b, conic_c = feature(slot, 2), feature(slot, 3), feature(slot, 4)
             results = [
                 conic_a * sum_x + conic_b * sum_y,
                 conic_b * sum_x + conic_c * sum_y,
-                -0.5 * total(flat * delta_x * delta_x),
-                -total(tilt * delta_x),
+                -0.5 * total(leaned[0] * delta_x[0] + leaned[1] * delta_x[1]),
+                -total(tilt[0] * delta_x[0] + tilt[1] * delta_x[1]),
                 -0.5 * total(bend),
-                total(flat),
+                total(flat[0] + flat[1]),
             ] + color_grads[tile]
-
-            @pl.when(entry >= 0)
-            def _():
-                for index in range(FEATS):
-                    out_ref[slot, :, index * BLOCK : (index + 1) * BLOCK] = results[index]
-
+            for index in range(FEATS):
+                out_ref[pl.ds(slot * FEATS + index, 1)] += results[index]
         return carry
 
-    lax.fori_loop(0, LIST, backward, 0)
+    lax.fori_loop(0, LIST, backward, 0, unroll=8)
 
 
 def collect_kernel(keys_ref, slots_ref, out_ref):
@@ -382,7 +404,10 @@
     codes = 2 * blocks_here
     rows = code_rows(params_ref, blocks_here)
     shift = code_shift(blocks_here)
-    cots = [cot_ref[codes * feat : codes * (feat + 1)] for feat in range(FEATS)]
+    summed = cot_ref[0]
+    for group in range(1, cot_ref.shape[0]):
+        summed = summed + cot_ref[group]
+    cots = [summed[codes * feat : codes * (feat + 1)] for feat in range(FEATS)]
     used = rows[:10] + rows[11:]
 
     def shown_of(values):
@@ -418,35 +443,34 @@
     return [pl.BlockSpec(memory_space=SMEM)] * count
 
 
-def on_device(params, adam_m, adam_v, target, tile_ids, send_blocks, tile_lists):
-    dev_count = lax.axis_size("dev")
-    g_local = params.shape[1]
-    blocks_here = g_local // BLOCK
+def run_project(params, provided, center_x, center_y, limit):
+    blocks_here = params.shape[1] // BLOCK
     codes = 2 * blocks_here
-    tiles_y = dev_count * blocks_here // TILES_X
-    center_x = 8.0 * TILES_X
-    center_y = 8.0 * tiles_y
-    tiles = tile_ids.shape[2]
     f32 = jnp.float32
-    limit = pltpu.CompilerParams(vmem_limit_bytes=VMEM_LIMIT)
-    provided = send_blocks.reshape(-1)
-    slot_shape = jax.ShapeDtypeStruct((dev_count, 1, SLOT), f32)
-
-    outgoing = pl.pallas_call(
+    return pl.pallas_call(
         lambda *refs: project_kernel(blocks_here, center_x, center_y, *refs),
-        out_shape=slot_shape,
-        in_specs=smem(1) + vmem(1),
+        out_shape=jax.ShapeDtypeStruct((provided.shape[0] * FEATS, BLOCK), f32),
+        in_specs=[pl.BlockSpec(memory_space=pltpu.MemorySpace.HBM)] * 2,
         out_specs=vmem(1)[0],
-        scratch_shapes=[pltpu.VMEM((codes, 1, SLOT), f32)],
+        scratch_shapes=[
+            pltpu.SMEM(provided.shape, jnp.int32),
+            pltpu.VMEM(params.shape, f32),
+            pltpu.VMEM((codes, FEATS, BLOCK), f32),
+            pltpu.SemaphoreType.DMA((2,)),
+        ],
         compiler_params=limit,
         name="project",
     )(provided, params)
-    incoming = lax.all_to_all(outgoing, "dev", split_axis=0, concat_axis=0, tiled=True)
+
+
+def run_render(scalars, incoming, goals, tiles_y, limit):
+    tiles = goals.shape[0]
+    f32 = jnp.float32
     pairs = pltpu.VMEM((tiles, LIST, TILE, BLOCK), f32)
-    cotangent = pl.pallas_call(
+    return pl.pallas_call(
         lambda *refs: render_kernel(tiles_y, *refs),
-        out_shape=slot_shape,
-        in_specs=smem(2) + vmem(2),
+        out_shape=jax.ShapeDtypeStruct(incoming.shape, f32),
+        in_specs=smem(1) + vmem(2),
         out_specs=vmem(1)[0],
         scratch_shapes=[
             pairs,
@@ -458,20 +482,23 @@
         ],
         compiler_params=limit,
         name="render",
-    )(tile_ids.reshape(-1), tile_lists.reshape(-1), incoming, target.reshape(target.shape[2:]))
-    returned = lax.all_to_all(cotangent, "dev", split_axis=0, concat_axis=0, tiled=True)
-    order = jnp.arange(FEATS, dtype=jnp.int32) * codes
-    keys = jnp.where(provided[:, None] >= 0, provided[:, None] + order[None, :], -1)
-    per_code = pl.pallas_call(
+    )(scalars, incoming, goals)
+
+
+def run_collect(keys, returned, codes, limit):
+    return pl.pallas_call(
         collect_kernel,
-        out_shape=jax.ShapeDtypeStruct((FEATS * codes, BLOCK), f32),
+        out_shape=jax.ShapeDtypeStruct((FEATS * codes, BLOCK), jnp.float32),
         in_specs=vmem(2),
         out_specs=vmem(1)[0],
         compiler_params=limit,
         name="collect",
-    )(keys.reshape(1, dev_count * FEATS), returned.reshape(dev_count * FEATS, BLOCK))
-    per_code = lax.psum(per_code, "rep")
-    shape = jax.ShapeDtypeStruct(params.shape, f32)
+    )(keys, returned)
+
+
+def run_update(gathered, params, adam_m, adam_v, center_x, center_y, limit):
+    blocks_here = params.shape[1] // BLOCK
+    shape = jax.ShapeDtypeStruct(params.shape, jnp.float32)
     return pl.pallas_call(
         lambda *refs: update_kernel(blocks_here, center_x, center_y, *refs),
         out_shape=(shape,) * 4,
@@ -479,7 +506,35 @@
         out_specs=tuple(vmem(4)),
         compiler_params=limit,
         name="update",
-    )(per_code, params, adam_m, adam_v)
+    )(gathered, params, adam_m, adam_v)
+
+
+def exchange(slots, dev_count):
+    sent = slots.reshape(dev_count, 1, SLOT)
+    return lax.all_to_all(sent, "dev", split_axis=0, concat_axis=0, tiled=True).reshape(slots.shape)
+
+
+def on_device(params, adam_m, adam_v, target, tile_ids, send_blocks, tile_lists):
+    dev_count = lax.axis_size("dev")
+    blocks_here = params.shape[1] // BLOCK
+    codes = 2 * blocks_here
+    tiles_y = dev_count * blocks_here // TILES_X
+    center_x = 8.0 * TILES_X
+    center_y = 8.0 * tiles_y
+    limit = pltpu.CompilerParams(vmem_limit_bytes=VMEM_LIMIT)
+    provided = send_blocks.reshape(-1)
+    scalars = jnp.concatenate([tile_ids.reshape(-1), tile_lists.reshape(-1)])
+
+    outgoing = run_project(params, provided, center_x, center_y, limit)
+    incoming = exchange(outgoing, dev_count)
+    goals = target.reshape(target.shape[2:])
+    cotangent = run_render(scalars, incoming, goals, tiles_y, limit)
+    returned = exchange(cotangent, dev_count)
+    order = jnp.arange(FEATS, dtype=jnp.int32) * codes
+    keys = jnp.where(provided[:, None] >= 0, provided[:, None] + order[None, :], -1)
+    per_code = run_collect(keys.reshape(1, dev_count * FEATS), returned, codes, limit)
+    gathered = lax.all_gather(per_code, "rep", axis=0, tiled=False)
+    return run_update(gathered, params, adam_m, adam_v, center_x, center_y, limit)
 
 
 def solution(mesh):

time: 129 us -> 123 us (0.953)
  blocking collectives: 17.6 us -> 12.7 us
    psum x1 -> x0, blocking collectives: 17.6 us -> none  [on_device(): per_code = lax.psum(per_code, 'rep')]
    all_gather x0 -> x1, blocking collectives: none -> 12.7 us  [on_device(): gathered = lax.all_gather(per_code, 'rep', axis=0, tiled=False)]
where the time goes in v2:
time: 123 us
  waiting for transfers between devices  69.4 us (56%)
  starting transfers between devices  26.5 us (22%)
  blocking collectives  12.7 us (10%)
  Pallas kernels  10.1 us (8%)
  local copies, waits for them, and re-layouts  3.18 us (3%)
    all_to_all x2, waiting for transfers between devices, exchange(): lax.all_to_all(sent, 'dev', split_axis=0, concat_axis=0, tiled=True)  69.4 us
    all_to_all x2, starting transfers between devices, exchange(): lax.all_to_all(sent, 'dev', split_axis=0, concat_axis=0, tiled=True)  26.5 us
    all_gather x1, blocking collectives, on_device(): gathered = lax.all_gather(per_code, 'rep', axis=0, tiled=False)  12.7 us
    pallas_call x1, Pallas kernels, run_render(): pl.pallas_call(lambda *refs: render_kernel(tiles_y, *refs), out_shape=jax...  6.89 us
    unnamed x17, local copies, waits for them, and re-layouts  2.89 us
  transfers between devices with their start and end apart: 2, of which 2 were waited for; matrix products, arithmetic and copies ran while one was open for 0% of the time, Pallas kernels for 0%

profile of v2, /device:TPU:6, one launch (start us, length us, event | category | flops | bytes accessed | tf_op | source)
XLA Modules:
  0.0 122.7 jit_solution(1985180971228545221)
XLA Ops:
  0.6 0.0 copy-start.4
  0.6 0.6 copy-done.4
  1.3 0.9 copy-done
  2.2 1.8 %project.1 = f32[1152,128]{1,0:T(8,128)} custom-call(s32[128]{0:T(128)S(1)} %bitcast.15, f32[59,512]{1,0:T(8,128)S(1)} %copy-done), custom_call_target="tpu_custom_call" | custom-call | tf_op jit(solution)/shard_map/project/pallas_call | solution.py:450
  4.0 0.0 copy-start.5
  4.0 19.4 %all-to-all-start = ((f32[128,1,1152]{2,1,0:T(1,128)}), f32[128,1,1152]{2,1,0:T(1,128)S(1)}, u32[]{:S(2)}, u32[]{:S(2)}) async-start(f32[128,1,1152]{2,1,0:T(1,128)} %bitcast.2), calls=%async_computation | async-start | bytes 1179648 | tf_op jit(solution)/shard_map/all_to_all | solution.py:514
  23.4 0.0 copy-done.5
  23.4 0.0 copy-start.6
  23.4 0.7 copy-done.6
  24.1 0.1 reshape.80
  24.2 0.7 copy-done.7
  24.8 0.1 pad_add_fusion.refs_0_
  24.9 34.1 %all-to-all-done = f32[128,1,1152]{2,1,0:T(1,128)S(1)} async-done(((f32[128,1,1152]{2,1,0:T(1,128)}), f32[128,1,1152]{2,1,0:T(1,128)S(1)}, u32[]{:S(2)}, u32[]{:S(2)}) %all-to-all-start) | async-done | bytes 589856 | tf_op jit(solution)/shard_map/all_to_all | solution.py:514
  59.0 6.9 %render.1 = f32[1152,128]{1,0:T(8,128)} custom-call(s32[18]{0:T(128)S(1)} %pad_add_fusion.refs_0_, f32[1152,128]{1,0:T(8,128)S(1)} %bitcast.12, f32[2,3,256]{2,1,0:T(4,128)S(1)} %bitcast.14), custom_call_target="tpu_custom_call" | custom-call | tf_op jit(solution)/shard_map/render/pallas_call | solution.py:470
  65.9 7.1 %all-to-all-start.1 = ((f32[128,1,1152]{2,1,0:T(1,128)}), f32[128,1,1152]{2,1,0:T(1,128)S(1)}, u32[]{:S(2)}, u32[]{:S(2)}) async-start(f32[128,1,1152]{2,1,0:T(1,128)} %bitcast.5), calls=%async_computation.1 | async-start | bytes 1179648 | tf_op jit(solution)/shard_map/all_to_all | solution.py:514
  73.0 0.1 add_select_fusion
  73.1 0.2 select_n.15.keys_ref
  73.3 35.3 %all-to-all-done.1 = f32[128,1,1152]{2,1,0:T(1,128)S(1)} async-done(((f32[128,1,1152]{2,1,0:T(1,128)}), f32[128,1,1152]{2,1,0:T(1,128)S(1)}, u32[]{:S(2)}, u32[]{:S(2)}) %all-to-all-start.1) | async-done | bytes 589856 | tf_op jit(solution)/shard_map/all_to_all | solution.py:514
  108.6 0.3 collect.1
  108.9 0.0 copy-start.1
  109.0 12.7 %all-gather = f32[288,128]{1,0:T(8,128)S(1)} all-gather(f32[72,128]{1,0:T(8,128)S(1)} %collect.1), channel_id=2, replica_groups=mesh['rep'=4,'dev'=128] {'rep'}, dimensions={0}, use_global_device_ids=true | all-gather | bytes 184320 | tf_op jit(solution)/shard_map/all_gather | solution.py:536
  121.6 0.0 copy-done.2
  121.6 0.0 copy-done.3
  121.7 1.1 update.1
  (8 shorter events, 0.0 us)
Async XLA Ops:
  0.6 0.7 copy-start.4
  1.3 0.9 copy-start
  4.0 19.4 %copy-start.5 = (f32[1,1,2,3,256]{4,2,3,1,0:T(2,128)S(1)}, f32[1,1,2,3,256]{4,2,3,1,0:T(2,128)}, u32[]{:S(2)}) copy-start(f32[1,1,2,3,256]{4,2,3,1,0:T(2,128)} %param.10) | copy-start | bytes 18436
  4.0 55.0 %all-to-all-start = ((f32[128,1,1152]{2,1,0:T(1,128)}), f32[128,1,1152]{2,1,0:T(1,128)S(1)}, u32[]{:S(2)}, u32[]{:S(2)}) async-start(f32[128,1,1152]{2,1,0:T(1,128)} %bitcast.2), calls=%async_computation | async-start | bytes 1179648 | tf_op jit(solution)/shard_map/all_to_all | solution.py:514
  23.4 0.7 copy-start.6
  24.2 0.7 copy-start.7
  65.9 42.7 %all-to-all-start.1 = ((f32[128,1,1152]{2,1,0:T(1,128)}), f32[128,1,1152]{2,1,0:T(1,128)S(1)}, u32[]{:S(2)}, u32[]{:S(2)}) async-start(f32[128,1,1152]{2,1,0:T(1,128)} %bitcast.5), calls=%async_computation.1 | async-start | bytes 1179648 | tf_op jit(solution)/shard_map/all_to_all | solution.py:514
  108.6 13.1 %copy-start.2 = (f32[59,512]{1,0:T(8,128)S(1)}, f32[59,512]{1,0:T(8,128)}, u32[]{:S(2)}) copy-start(f32[59,512]{1,0:T(8,128)} %refs_2_.1) | copy-start | bytes 362500
  108.6 13.1 %copy-start.3 = (f32[59,512]{1,0:T(8,128)S(1)}, f32[59,512]{1,0:T(8,128)}, u32[]{:S(2)}) copy-start(f32[59,512]{1,0:T(8,128)} %refs_3_.1) | copy-start | bytes 362500
  108.9 12.7 %copy-start.1 = (f32[59,512]{1,0:T(8,128)S(1)}, f32[59,512]{1,0:T(8,128)}, u32[]{:S(2)}) copy-start(f32[59,512]{1,0:T(8,128)} %refs_1_.3) | copy-start | bytes 362500

commit v3 on v2

--- a/solution.py
+++ b/solution.py
@@ -44,6 +44,7 @@
 RATES = [(0, 0.00016), (3, 0.005), (6, 0.001), (10, 0.05), (11, 0.0025), (14, 0.000125)]
 
 VMEM_LIMIT = 40 * 1024 * 1024
+WHOLE_VMEM = 60 * 1024 * 1024
 SMEM = pltpu.MemorySpace.SMEM
 VMEM = pltpu.MemorySpace.VMEM
 
@@ -379,13 +380,15 @@
 
 
 def collect_kernel(keys_ref, slots_ref, out_ref):
-    count, width = out_ref.shape[0], slots_ref.shape[0]
+    copies, count = out_ref.shape[:2]
+    width = slots_ref.shape[0]
     wanted = lax.broadcasted_iota(jnp.int32, (count, width), 0)
     picker = jnp.where(keys_ref[...] == wanted, 1.0, 0.0).astype(jnp.bfloat16)
-    total = jnp.zeros(out_ref.shape, jnp.float32)
+    total = jnp.zeros((count, BLOCK), jnp.float32)
     for piece in halves(slots_ref[...], 3):
         total += jnp.dot(picker, piece, preferred_element_type=jnp.float32)
-    out_ref[...] = total
+    for copy in range(copies):
+        out_ref[copy] = total
 
 
 def update_kernel(
@@ -458,7 +461,7 @@
             pltpu.VMEM((codes, FEATS, BLOCK), f32),
             pltpu.SemaphoreType.DMA((2,)),
         ],
-        compiler_params=limit,
+        compiler_params=pltpu.CompilerParams(vmem_limit_bytes=WHOLE_VMEM),
         name="project",
     )(provided, params)
 
@@ -485,10 +488,10 @@
     )(scalars, incoming, goals)
 
 
-def run_collect(keys, returned, codes, limit):
+def run_collect(keys, returned, codes, groups, limit):
     return pl.pallas_call(
         collect_kernel,
-        out_shape=jax.ShapeDtypeStruct((FEATS * codes, BLOCK), jnp.float32),
+        out_shape=jax.ShapeDtypeStruct((groups, FEATS * codes, BLOCK), jnp.float32),
         in_specs=vmem(2),
         out_specs=vmem(1)[0],
         compiler_params=limit,
@@ -532,8 +535,10 @@
     returned = exchange(cotangent, dev_count)
     order = jnp.arange(FEATS, dtype=jnp.int32) * codes
     keys = jnp.where(provided[:, None] >= 0, provided[:, None] + order[None, :], -1)
-    per_code = run_collect(keys.reshape(1, dev_count * FEATS), returned, codes, limit)
-    gathered = lax.all_gather(per_code, "rep", axis=0, tiled=False)
+    groups = lax.axis_size("rep")
+    keys = keys.reshape(1, dev_count * FEATS)
+    per_code = run_collect(keys, returned, codes, groups, limit)
+    gathered = lax.all_to_all(per_code, "rep", split_axis=0, concat_axis=0, tiled=True)
     return run_update(gathered, params, adam_m, adam_v, center_x, center_y, limit)
 
 

time: 123 us -> 120 us (0.976)
  blocking collectives: 12.7 us -> 10.4 us
    all_gather x1 -> x0, blocking collectives: 12.7 us -> none  [on_device(): gathered = lax.all_gather(per_code, 'rep', axis=0, tiled=False)]
    all_to_all x0 -> x1, blocking collectives: none -> 10.4 us  [on_device(): lax.all_to_all(per_code, 'rep', split_axis=0, concat_axis=0, tiled=True)]
    unnamed x17 -> x15, local copies, waits for them, and re-layouts: 2.89 us -> 1.98 us
where the time goes in v3:
time: 120 us; the launch traced here: 119 us
  waiting for transfers between devices  68.7 us (57%)
  starting transfers between devices  26.5 us (22%)
  Pallas kernels  10.5 us (9%)
  blocking collectives  10.4 us (9%)
  local copies, waits for them, and re-layouts  2.27 us (2%)
    all_to_all x2, waiting for transfers between devices, exchange(): lax.all_to_all(sent, 'dev', split_axis=0, concat_axis=0, tiled=True)  68.7 us
    all_to_all x2, starting transfers between devices, exchange(): lax.all_to_all(sent, 'dev', split_axis=0, concat_axis=0, tiled=True)  26.5 us
    all_to_all x1, blocking collectives, on_device(): lax.all_to_all(per_code, 'rep', split_axis=0, concat_axis=0, tiled=True)  10.4 us
    pallas_call x1, Pallas kernels, run_render(): pl.pallas_call(lambda *refs: render_kernel(tiles_y, *refs), out_shape=jax...  6.88 us
  transfers between devices with their start and end apart: 2, of which 2 were waited for; matrix products, arithmetic and copies ran while one was open for 0% of the time, Pallas kernels for 0%

profile of v3, /device:TPU:6, one launch (start us, length us, event | category | flops | bytes accessed | tf_op | source)
XLA Modules:
  0.0 119.3 jit_solution(875979912619335179)
XLA Ops:
  0.6 2.2 %project.1 = f32[1152,128]{1,0:T(8,128)} custom-call(s32[128]{0:T(128)} %bitcast.14, f32[59,512]{1,0:T(8,128)} %refs_1_.3), custom_call_target="tpu_custom_call" | custom-call | tf_op jit(solution)/shard_map/project/pallas_call | solution.py:453
  2.8 0.0 copy-start.3
  2.8 19.4 %all-to-all-start = ((f32[128,1,1152]{2,1,0:T(1,128)}), f32[128,1,1152]{2,1,0:T(1,128)S(1)}, u32[]{:S(2)}, u32[]{:S(2)}) async-start(f32[128,1,1152]{2,1,0:T(1,128)} %bitcast.13), calls=%async_computation | async-start | bytes 1179648 | tf_op jit(solution)/shard_map/all_to_all | solution.py:517
  22.2 0.0 copy-done.3
  22.2 0.0 copy-start.5
  22.2 0.7 copy-done.5
  22.9 0.1 reshape.80
  23.0 0.7 copy-done.6
  23.6 0.1 pad_add_fusion.refs_0_
  23.7 34.1 %all-to-all-done = f32[128,1,1152]{2,1,0:T(1,128)S(1)} async-done(((f32[128,1,1152]{2,1,0:T(1,128)}), f32[128,1,1152]{2,1,0:T(1,128)S(1)}, u32[]{:S(2)}, u32[]{:S(2)}) %all-to-all-start) | async-done | bytes 589856 | tf_op jit(solution)/shard_map/all_to_all | solution.py:517
  57.8 6.9 %render.1 = f32[1152,128]{1,0:T(8,128)} custom-call(s32[18]{0:T(128)S(1)} %pad_add_fusion.refs_0_, f32[1152,128]{1,0:T(8,128)S(1)} %bitcast.11, f32[2,3,256]{2,1,0:T(4,128)S(1)} %bitcast.12), custom_call_target="tpu_custom_call" | custom-call | tf_op jit(solution)/shard_map/render/pallas_call | solution.py:473
  64.7 7.1 %all-to-all-start.1 = ((f32[128,1,1152]{2,1,0:T(1,128)}), f32[128,1,1152]{2,1,0:T(1,128)S(1)}, u32[]{:S(2)}, u32[]{:S(2)}) async-start(f32[128,1,1152]{2,1,0:T(1,128)} %bitcast.5), calls=%async_computation.1 | async-start | bytes 1179648 | tf_op jit(solution)/shard_map/all_to_all | solution.py:517
  71.8 0.0 copy-start.4
  71.8 0.6 copy-done.4
  72.5 0.1 add_select_fusion
  72.6 0.2 select_n.15.keys_ref
  72.8 34.6 %all-to-all-done.1 = f32[128,1,1152]{2,1,0:T(1,128)S(1)} async-done(((f32[128,1,1152]{2,1,0:T(1,128)}), f32[128,1,1152]{2,1,0:T(1,128)S(1)}, u32[]{:S(2)}, u32[]{:S(2)}) %all-to-all-start.1) | async-done | bytes 589856 | tf_op jit(solution)/shard_map/all_to_all | solution.py:517
  107.4 0.3 collect.1
  107.8 0.0 copy-start
  107.8 0.0 copy-start.1
  107.8 10.4 %all_to_all.15.refs_0_ = f32[4,72,128]{2,1,0:T(8,128)S(1)} all-to-all(f32[4,72,128]{2,1,0:T(8,128)S(1)} %collect.1), channel_id=1, replica_groups=mesh['rep'=4,'dev'=128] {'rep'}, dimensions={0} | all-to-all | bytes 294912 | tf_op jit(solution)/shard_map/all_to_all | solution.py:541
  118.2 0.0 copy-done.2
  118.2 0.0 copy-done
  118.2 1.1 update.1
  (6 shorter events, 0.0 us)
Async XLA Ops:
  2.8 19.4 %copy-start.3 = (f32[1,1,2,3,256]{4,2,3,1,0:T(2,128)S(1)}, f32[1,1,2,3,256]{4,2,3,1,0:T(2,128)}, u32[]{:S(2)}) copy-start(f32[1,1,2,3,256]{4,2,3,1,0:T(2,128)} %param.10) | copy-start | bytes 18436
  2.8 55.0 %all-to-all-start = ((f32[128,1,1152]{2,1,0:T(1,128)}), f32[128,1,1152]{2,1,0:T(1,128)S(1)}, u32[]{:S(2)}, u32[]{:S(2)}) async-start(f32[128,1,1152]{2,1,0:T(1,128)} %bitcast.13), calls=%async_computation | async-start | bytes 1179648 | tf_op jit(solution)/shard_map/all_to_all | solution.py:517
  22.2 0.7 copy-start.5
  23.0 0.7 copy-start.6
  64.7 42.7 %all-to-all-start.1 = ((f32[128,1,1152]{2,1,0:T(1,128)}), f32[128,1,1152]{2,1,0:T(1,128)S(1)}, u32[]{:S(2)}, u32[]{:S(2)}) async-start(f32[128,1,1152]{2,1,0:T(1,128)} %bitcast.5), calls=%async_computation.1 | async-start | bytes 1179648 | tf_op jit(solution)/shard_map/all_to_all | solution.py:517
  71.8 0.7 copy-start.4
  107.4 10.8 %copy-start.2 = (f32[59,512]{1,0:T(8,128)S(1)}, f32[59,512]{1,0:T(8,128)}, u32[]{:S(2)}) copy-start(f32[59,512]{1,0:T(8,128)} %refs_3_.1) | copy-start | bytes 362500
  107.8 10.5 %copy-start = (f32[59,512]{1,0:T(8,128)S(1)}, f32[59,512]{1,0:T(8,128)}, u32[]{:S(2)}) copy-start(f32[59,512]{1,0:T(8,128)} %refs_1_.3) | copy-start | bytes 362500
  107.8 10.5 %copy-start.1 = (f32[59,512]{1,0:T(8,128)S(1)}, f32[59,512]{1,0:T(8,128)}, u32[]{:S(2)}) copy-start(f32[59,512]{1,0:T(8,128)} %refs_2_.1) | copy-start | bytes 362500

commit v4 on v3

--- a/solution.py
+++ b/solution.py
@@ -12,6 +12,7 @@
 TILE = 256
 SIDE = 16
 LIST = 8
+OUT_PARTS = 4
 TILES_X = 64
 ADAM_STEP = 1000
 
@@ -177,22 +178,36 @@
 
 
 def project_kernel(
-    blocks_here, center_x, center_y, codes_hbm, params_hbm, out_ref, codes_ref, params_ref, table_ref, sems
+    blocks_here,
+    center_x,
+    center_y,
+    codes_hbm,
+    params_hbm,
+    out_hbm,
+    codes_ref,
+    params_ref,
+    table_ref,
+    out_ref,
+    sems,
+    out_sems,
 ):
-    copies = [
-        pltpu.make_async_copy(params_hbm, params_ref, sems.at[0]),
-        pltpu.make_async_copy(codes_hbm, codes_ref, sems.at[1]),
-    ]
+    copies = [pltpu.make_async_copy(codes_hbm, codes_ref, sems.at[blocks_here])]
+    for block in range(blocks_here):
+        where = (slice(None), pl.ds(block * BLOCK, BLOCK))
+        copies.append(
+            pltpu.make_async_copy(params_hbm.at[where], params_ref.at[where], sems.at[block])
+        )
     for copy in copies:
         copy.start()
-    copies[0].wait()
+    for copy in copies[1:]:
+        copy.wait()
     rows = code_rows(params_ref, blocks_here)
     shown = project(rows, code_shift(blocks_here), center_x, center_y)
     shown = shown[:5] + [jax.nn.sigmoid(rows[10])] + shown[5:]
     for code in range(2 * blocks_here):
         for feat in range(FEATS):
             table_ref[code, feat : feat + 1] = shown[feat][code : code + 1]
-    copies[1].wait()
+    copies[0].wait()
 
     def fill(target, carry):
         code = jnp.maximum(codes_ref[target], 0)
@@ -200,7 +215,18 @@
         out_ref[pl.ds(target * FEATS + 8, 1)] = table_ref[code, 8:9]
         return carry
 
-    lax.fori_loop(0, out_ref.shape[0] // FEATS, fill, 0, unroll=8)
+    rows = out_ref.shape[0] // OUT_PARTS
+    parts = []
+    for index in range(OUT_PARTS):
+        first = index * (rows // FEATS)
+        lax.fori_loop(first, first + rows // FEATS, fill, 0, unroll=32)
+        where = pl.ds(index * rows, rows)
+        parts.append(
+            pltpu.make_async_copy(out_ref.at[where], out_hbm.at[where], out_sems.at[index])
+        )
+        parts[-1].start()
+    for part in parts:
+        part.wait()
 
 
 def render_kernel(
@@ -262,7 +288,17 @@
             pieces_ref[start : start + SIDE, side * BLOCK : (side + 1) * BLOCK] = both
 
     def add_up(matrix):
-        return jnp.dot(pieces_ref[...], matrix, preferred_element_type=f32)
+        return jnp.concatenate(
+            [
+                jnp.dot(
+                    pieces_ref[tile * TILE : (tile + 1) * TILE],
+                    matrix,
+                    preferred_element_type=f32,
+                )
+                for tile in range(tiles)
+            ],
+            axis=0,
+        )
 
     def forward(layer, carry):
         for tile in range(tiles):
@@ -454,12 +490,14 @@
         lambda *refs: project_kernel(blocks_here, center_x, center_y, *refs),
         out_shape=jax.ShapeDtypeStruct((provided.shape[0] * FEATS, BLOCK), f32),
         in_specs=[pl.BlockSpec(memory_space=pltpu.MemorySpace.HBM)] * 2,
-        out_specs=vmem(1)[0],
+        out_specs=pl.BlockSpec(memory_space=pl.ANY),
         scratch_shapes=[
             pltpu.SMEM(provided.shape, jnp.int32),
             pltpu.VMEM(params.shape, f32),
             pltpu.VMEM((codes, FEATS, BLOCK), f32),
-            pltpu.SemaphoreType.DMA((2,)),
+            pltpu.VMEM((provided.shape[0] * FEATS, BLOCK), f32),
+            pltpu.SemaphoreType.DMA((blocks_here + 1,)),
+            pltpu.SemaphoreType.DMA((OUT_PARTS,)),
         ],
         compiler_params=pltpu.CompilerParams(vmem_limit_bytes=WHOLE_VMEM),
         name="project",
@@ -527,16 +565,17 @@
     limit = pltpu.CompilerParams(vmem_limit_bytes=VMEM_LIMIT)
     provided = send_blocks.reshape(-1)
     scalars = jnp.concatenate([tile_ids.reshape(-1), tile_lists.reshape(-1)])
+    order = jnp.arange(FEATS, dtype=jnp.int32) * codes
+    keys = jnp.where(provided[:, None] >= 0, provided[:, None] + order[None, :], -1)
+    keys = keys.reshape(1, dev_count * FEATS)
+    scalars, keys = lax.optimization_barrier((scalars, keys))
 
     outgoing = run_project(params, provided, center_x, center_y, limit)
     incoming = exchange(outgoing, dev_count)
     goals = target.reshape(target.shape[2:])
     cotangent = run_render(scalars, incoming, goals, tiles_y, limit)
     returned = exchange(cotangent, dev_count)
-    order = jnp.arange(FEATS, dtype=jnp.int32) * codes
-    keys = jnp.where(provided[:, None] >= 0, provided[:, None] + order[None, :], -1)
     groups = lax.axis_size("rep")
-    keys = keys.reshape(1, dev_count * FEATS)
     per_code = run_collect(keys, returned, codes, groups, limit)
     gathered = lax.all_to_all(per_code, "rep", split_axis=0, concat_axis=0, tiled=True)
     return run_update(gathered, params, adam_m, adam_v, center_x, center_y, limit)

time: 120 us -> 118 us (0.983)
  blocking collectives: 10.4 us -> 53 us
  waiting for transfers between devices: 68.7 us -> 33.8 us
  starting transfers between devices: 26.5 us -> 19.4 us
  Pallas kernels: 10.5 us -> 9.29 us
    all_to_all x0 -> x1, blocking collectives: none -> 42.5 us  [exchange(): lax.all_to_all(sent, 'dev', split_axis=0, concat_axis=0, tiled=True)]
    all_to_all x2 -> x1, waiting for transfers between devices: 68.7 us -> 33.8 us  [exchange(): lax.all_to_all(sent, 'dev', split_axis=0, concat_axis=0, tiled=True)]
    all_to_all x2 -> x1, starting transfers between devices: 26.5 us -> 19.4 us  [exchange(): lax.all_to_all(sent, 'dev', split_axis=0, concat_axis=0, tiled=True)]
  transfers between devices with their start and end apart: 2 -> 1, of which waited for: 2 -> 1; matrix products, arithmetic and copies ran while one was open for 0% -> 0% of each run, Pallas kernels for 0% -> 0%
where the time goes in v4:
time: 118 us
  blocking collectives  53 us (45%)
  waiting for transfers between devices  33.8 us (29%)
  starting transfers between devices  19.4 us (16%)
  Pallas kernels  9.29 us (8%)
  local copies, waits for them, and re-layouts  1.62 us (1%)
    all_to_all x1, blocking collectives, exchange(): lax.all_to_all(sent, 'dev', split_axis=0, concat_axis=0, tiled=True)  42.5 us
    all_to_all x1, waiting for transfers between devices, exchange(): lax.all_to_all(sent, 'dev', split_axis=0, concat_axis=0, tiled=True)  33.8 us
    all_to_all x1, starting transfers between devices, exchange(): lax.all_to_all(sent, 'dev', split_axis=0, concat_axis=0, tiled=True)  19.4 us
    all_to_all x1, blocking collectives, on_device(): lax.all_to_all(per_code, 'rep', split_axis=0, concat_axis=0, tiled=True)  10.4 us
    pallas_call x1, Pallas kernels, run_render(): pl.pallas_call(lambda *refs: render_kernel(tiles_y, *refs), out_shape=jax...  6.01 us
  transfers between devices with their start and end apart: 1, of which 1 were waited for; matrix products, arithmetic and copies ran while one was open for 0% of the time, Pallas kernels for 0%

profile of v4, /device:TPU:6, one launch (start us, length us, event | category | flops | bytes accessed | tf_op | source)
XLA Modules:
  0.0 117.9 jit_solution(11607452442549184781)
XLA Ops:
  0.6 1.9 %project.1 = f32[1152,128]{1,0:T(8,128)} custom-call(s32[128]{0:T(128)} %bitcast.15, f32[59,512]{1,0:T(8,128)} %refs_1_.3), custom_call_target="tpu_custom_call" | custom-call | tf_op jit(solution)/shard_map/project/pallas_call | solution.py:489
  2.5 0.0 copy-start.5
  2.5 19.4 %all-to-all-start = ((f32[128,1,1152]{2,1,0:T(1,128)}), f32[128,1,1152]{2,1,0:T(1,128)S(1)}, u32[]{:S(2)}, u32[]{:S(2)}) async-start(f32[128,1,1152]{2,1,0:T(1,128)} %bitcast.14), calls=%async_computation | async-start | bytes 1179648 | tf_op jit(solution)/shard_map/all_to_all | solution.py:555
  21.9 0.0 copy-done.5
  21.9 0.1 reshape.80
  22.0 0.7 copy-done.4
  22.7 0.1 add_select_fusion
  22.8 0.0 copy-start.3
  22.8 0.2 select_n.15.keys_ref
  23.0 0.0 copy-start.6
  23.0 0.6 copy-done.6
  23.7 0.1 pad_add_fusion.refs_0_
  23.7 0.0 copy-done.3
  23.7 33.8 %all-to-all-done = f32[128,1,1152]{2,1,0:T(1,128)S(1)} async-done(((f32[128,1,1152]{2,1,0:T(1,128)}), f32[128,1,1152]{2,1,0:T(1,128)S(1)}, u32[]{:S(2)}, u32[]{:S(2)}) %all-to-all-start) | async-done | bytes 589856 | tf_op jit(solution)/shard_map/all_to_all | solution.py:555
  57.5 6.0 %render.1 = f32[1152,128]{1,0:T(8,128)S(1)} custom-call(s32[18]{0:T(128)S(1)} %pad_add_fusion.refs_0_, f32[1152,128]{1,0:T(8,128)S(1)} %bitcast.10, f32[2,3,256]{2,1,0:T(4,128)S(1)} %bitcast.13), custom_call_target="tpu_custom_call" | custom-call | tf_op jit(solution)/shard_map/render/pallas_call | solution.py:511
  63.5 42.5 %all_to_all.15 = f32[128,1,1152]{2,1,0:T(1,128)S(1)} all-to-all(f32[128,1,1152]{2,1,0:T(1,128)S(1)} %bitcast.11), channel_id=1, replica_groups=mesh['rep'=4,'dev'=128] {'dev'}, dimensions={0} | all-to-all | bytes 1179648 | tf_op jit(solution)/shard_map/all_to_all | solution.py:555
  106.0 0.3 collect.1
  106.4 0.0 copy-start
  106.4 0.0 copy-start.1
  106.4 10.4 %all_to_all.16.refs_0_ = f32[4,72,128]{2,1,0:T(8,128)S(1)} all-to-all(f32[4,72,128]{2,1,0:T(8,128)S(1)} %collect.1), channel_id=1, replica_groups=mesh['rep'=4,'dev'=128] {'rep'}, dimensions={0} | all-to-all | bytes 294912 | tf_op jit(solution)/shard_map/all_to_all | solution.py:580
  116.9 0.0 copy-done.2
  116.9 0.0 copy-done
  116.9 0.0 copy-done.1
  116.9 1.1 update.1
  (5 shorter events, 0.0 us)
Async XLA Ops:
  2.5 19.4 %copy-start.5 = (s32[1,1,2,8]{3,2,1,0:T(2,128)S(1)}, s32[1,1,2,8]{3,2,1,0:T(2,128)}, u32[]{:S(2)}) copy-start(s32[1,1,2,8]{3,2,1,0:T(2,128)} %param.13) | copy-start | bytes 196
  2.5 55.0 %all-to-all-start = ((f32[128,1,1152]{2,1,0:T(1,128)}), f32[128,1,1152]{2,1,0:T(1,128)S(1)}, u32[]{:S(2)}, u32[]{:S(2)}) async-start(f32[128,1,1152]{2,1,0:T(1,128)} %bitcast.14), calls=%async_computation | async-start | bytes 1179648 | tf_op jit(solution)/shard_map/all_to_all | solution.py:555
  22.0 0.7 copy-start.4
  22.8 1.0 copy-start.3
  23.0 0.7 copy-start.6
  106.0 10.8 %copy-start.2 = (f32[59,512]{1,0:T(8,128)S(1)}, f32[59,512]{1,0:T(8,128)}, u32[]{:S(2)}) copy-start(f32[59,512]{1,0:T(8,128)} %refs_3_.1) | copy-start | bytes 362500
  106.4 10.5 %copy-start = (f32[59,512]{1,0:T(8,128)S(1)}, f32[59,512]{1,0:T(8,128)}, u32[]{:S(2)}) copy-start(f32[59,512]{1,0:T(8,128)} %refs_1_.3) | copy-start | bytes 362500
  106.4 10.5 %copy-start.1 = (f32[59,512]{1,0:T(8,128)S(1)}, f32[59,512]{1,0:T(8,128)}, u32[]{:S(2)}) copy-start(f32[59,512]{1,0:T(8,128)} %refs_2_.1) | copy-start | bytes 362500

commit v5 on v4

--- a/solution.py
+++ b/solution.py
@@ -12,6 +12,7 @@
 TILE = 256
 SIDE = 16
 LIST = 8
+LOG2_E = 1.4426950408889634
 OUT_PARTS = 4
 TILES_X = 64
 ADAM_STEP = 1000
@@ -306,17 +307,21 @@
             slot = jnp.maximum(entry, 0)
             live = jnp.where(entry >= 0, 1.0, 0.0).astype(f32)
             delta_x, place_y = offsets(tile, slot)
-            half_x = [wide(-0.5 * feature(slot, 2)) * delta * delta for delta in delta_x]
-            cross = [wide(-feature(slot, 3)) * delta for delta in delta_x]
-            half_y = wide(-0.5 * feature(slot, 4))
-            opacity = wide(feature(slot, 5) * live)
+            scale = jnp.float32(LOG2_E)
+            brightness = wide(jnp.log(feature(slot, 5) * live) * scale)
+            half_x = [
+                wide((-0.5 * scale) * feature(slot, 2)) * delta * delta + brightness
+                for delta in delta_x
+            ]
+            cross = [wide(-scale * feature(slot, 3)) * delta for delta in delta_x]
+            half_y = wide((-0.5 * scale) * feature(slot, 4))
             for row in range(SIDE):
                 delta_y = (row - (SIDE / 2 - 0.5)) - place_y
                 scaled_y = half_y * delta_y
                 logs = []
                 for part in range(2):
                     power = half_x[part] + delta_y * (cross[part] + scaled_y)
-                    alpha = opacity * jnp.exp(power)
+                    alpha = jnp.exp2(power)
                     alpha_ref[tile, layer, row_of(row, part)] = alpha
                     logs.append(jnp.log(1.0 - alpha))
                 split_row(tile, row, logs)

time: 118 us -> 118 us (level)
  no operation moved by 1% of the time
where the time goes in v5:
time: 118 us
  blocking collectives  53 us (45%)
  waiting for transfers between devices  33.8 us (29%)
  starting transfers between devices  19.4 us (16%)
  Pallas kernels  9.15 us (8%)
  local copies, waits for them, and re-layouts  1.62 us (1%)
    all_to_all x1, blocking collectives, exchange(): lax.all_to_all(sent, 'dev', split_axis=0, concat_axis=0, tiled=True)  42.5 us
    all_to_all x1, waiting for transfers between devices, exchange(): lax.all_to_all(sent, 'dev', split_axis=0, concat_axis=0, tiled=True)  33.8 us
    all_to_all x1, starting transfers between devices, exchange(): lax.all_to_all(sent, 'dev', split_axis=0, concat_axis=0, tiled=True)  19.4 us
    all_to_all x1, blocking collectives, on_device(): lax.all_to_all(per_code, 'rep', split_axis=0, concat_axis=0, tiled=True)  10.5 us
    pallas_call x1, Pallas kernels, run_render(): pl.pallas_call(lambda *refs: render_kernel(tiles_y, *refs), out_shape=jax...  5.86 us
  transfers between devices with their start and end apart: 1, of which 1 were waited for; matrix products, arithmetic and copies ran while one was open for 0% of the time, Pallas kernels for 0%

profile of v5, /device:TPU:6, one launch (start us, length us, event | category | flops | bytes accessed | tf_op | source)
XLA Modules:
  0.0 117.8 jit_solution(13370276299777321312)
XLA Ops:
  0.6 1.9 %project.1 = f32[1152,128]{1,0:T(8,128)} custom-call(s32[128]{0:T(128)} %bitcast.15, f32[59,512]{1,0:T(8,128)} %refs_1_.3), custom_call_target="tpu_custom_call" | custom-call | tf_op jit(solution)/shard_map/project/pallas_call | solution.py:494
  2.5 0.0 copy-start.5
  2.5 19.4 %all-to-all-start = ((f32[128,1,1152]{2,1,0:T(1,128)}), f32[128,1,1152]{2,1,0:T(1,128)S(1)}, u32[]{:S(2)}, u32[]{:S(2)}) async-start(f32[128,1,1152]{2,1,0:T(1,128)} %bitcast.14), calls=%async_computation | async-start | bytes 1179648 | tf_op jit(solution)/shard_map/all_to_all | solution.py:560
  21.9 0.0 copy-done.5
  21.9 0.1 reshape.80
  22.0 0.7 copy-done.4
  22.7 0.1 add_select_fusion
  22.8 0.0 copy-start.3
  22.8 0.2 select_n.15.keys_ref
  23.0 0.0 copy-start.6
  23.0 0.6 copy-done.6
  23.7 0.1 pad_add_fusion.refs_0_
  23.7 0.0 copy-done.3
  23.7 33.8 %all-to-all-done = f32[128,1,1152]{2,1,0:T(1,128)S(1)} async-done(((f32[128,1,1152]{2,1,0:T(1,128)}), f32[128,1,1152]{2,1,0:T(1,128)S(1)}, u32[]{:S(2)}, u32[]{:S(2)}) %all-to-all-start) | async-done | bytes 589856 | tf_op jit(solution)/shard_map/all_to_all | solution.py:560
  57.5 5.9 %render.1 = f32[1152,128]{1,0:T(8,128)S(1)} custom-call(s32[18]{0:T(128)S(1)} %pad_add_fusion.refs_0_, f32[1152,128]{1,0:T(8,128)S(1)} %bitcast.10, f32[2,3,256]{2,1,0:T(4,128)S(1)} %bitcast.13), custom_call_target="tpu_custom_call" | custom-call | tf_op jit(solution)/shard_map/render/pallas_call | solution.py:516
  63.4 42.5 %all_to_all.15 = f32[128,1,1152]{2,1,0:T(1,128)S(1)} all-to-all(f32[128,1,1152]{2,1,0:T(1,128)S(1)} %bitcast.11), channel_id=1, replica_groups=mesh['rep'=4,'dev'=128] {'dev'}, dimensions={0} | all-to-all | bytes 1179648 | tf_op jit(solution)/shard_map/all_to_all | solution.py:560
  105.9 0.3 collect.1
  106.2 0.0 copy-start
  106.2 0.0 copy-start.1
  106.3 10.5 %all_to_all.16.refs_0_ = f32[4,72,128]{2,1,0:T(8,128)S(1)} all-to-all(f32[4,72,128]{2,1,0:T(8,128)S(1)} %collect.1), channel_id=1, replica_groups=mesh['rep'=4,'dev'=128] {'rep'}, dimensions={0} | all-to-all | bytes 294912 | tf_op jit(solution)/shard_map/all_to_all | solution.py:585
  116.7 0.0 copy-done.2
  116.7 0.0 copy-done
  116.7 0.0 copy-done.1
  116.7 1.1 update.1
  (5 shorter events, 0.0 us)
Async XLA Ops:
  2.5 19.4 %copy-start.5 = (s32[1,1,2,8]{3,2,1,0:T(2,128)S(1)}, s32[1,1,2,8]{3,2,1,0:T(2,128)}, u32[]{:S(2)}) copy-start(s32[1,1,2,8]{3,2,1,0:T(2,128)} %param.13) | copy-start | bytes 196
  2.5 55.0 %all-to-all-start = ((f32[128,1,1152]{2,1,0:T(1,128)}), f32[128,1,1152]{2,1,0:T(1,128)S(1)}, u32[]{:S(2)}, u32[]{:S(2)}) async-start(f32[128,1,1152]{2,1,0:T(1,128)} %bitcast.14), calls=%async_computation | async-start | bytes 1179648 | tf_op jit(solution)/shard_map/all_to_all | solution.py:560
  22.0 0.7 copy-start.4
  22.8 1.0 copy-start.3
  23.0 0.7 copy-start.6
  105.9 10.8 %copy-start.2 = (f32[59,512]{1,0:T(8,128)S(1)}, f32[59,512]{1,0:T(8,128)}, u32[]{:S(2)}) copy-start(f32[59,512]{1,0:T(8,128)} %refs_3_.1) | copy-start | bytes 362500
  106.2 10.5 %copy-start = (f32[59,512]{1,0:T(8,128)S(1)}, f32[59,512]{1,0:T(8,128)}, u32[]{:S(2)}) copy-start(f32[59,512]{1,0:T(8,128)} %refs_1_.3) | copy-start | bytes 362500
  106.2 10.5 %copy-start.1 = (f32[59,512]{1,0:T(8,128)S(1)}, f32[59,512]{1,0:T(8,128)}, u32[]{:S(2)}) copy-start(f32[59,512]{1,0:T(8,128)} %refs_2_.1) | copy-start | bytes 362500
